TPU v7x, 256 devices: a whole 4x4x8 slice. The times are simulated.
256 devices in a mesh: section: 16 (over x_lo, z), dp: 16 (over x_hi, y, core).
Axes of the slice: x: 4 (x_hi: 2, x_lo: 2; x = x_hi * 2 + x_lo), y: 4, z: 8, core: 2. Of those that a mesh axis runs over, the one named last changes fastest.
Arguments:
- activations: bfloat16 [16, 64, 64, 8192], P('section', 'dp'), may hold values from -6 to 6
- out_grads: bfloat16 [16, 64, 64, 8192], P('section', 'dp'), may hold values from -6 to 6
- proj_in: bfloat16 [16, 64, 8192], P('section'), may hold values from -0.0625 to 0.0625
- proj_out: bfloat16 [16, 64, 8192], P('section'), may hold values from -0.0625 to 0.0625
- queries: bfloat16 [16, 256, 4096], P('section', 'dp'), may hold values from -6 to 6
- lengths: int32 [16, 4], P('dp'), may hold values from 1 to 64, 160 in all within a row
Outputs:
- scores: float32 [64, 256], P('dp')
Inputs may be any that keep to these rules, and one draw needn't show every extreme that they name: `lengths`: the 4 examples of each data group use 5 * 32 tokens together, and one of them all 64.
All inputs are finite; a program needn't handle non-finite values.
Results may differ from a plain program's by a relative error of at most 0.005.
Values may be sent and summed in bfloat16 or wider, within the bound.
No kernel may reach another device: no remote copies, remote signals or barrier semaphores. Data moves between devices by JAX's collectives and lax.ppermute only.
A program may use at most 64 MiB of HBM per device.

v0:
```python
import jax
import jax.numpy as jnp
from jax import lax
from jax.sharding import PartitionSpec as P


def body(activations, out_grads, proj_in, proj_out, queries, lengths):
    layer_acts = activations[0]
    layer_grads = out_grads[0]
    examples_here = layer_acts.shape[0]
    seq_slots = layer_acts.shape[1]
    width = layer_acts.shape[2]
    rank = proj_in.shape[1]
    lengths_flat = lengths.reshape(-1)
    positions = jnp.arange(seq_slots, dtype=jnp.int32)
    token_mask = (positions[None, :] < lengths_flat[:, None]).astype(jnp.bfloat16)
    in_coords = jnp.dot(
        layer_acts.reshape(-1, width), proj_in[0].T, preferred_element_type=jnp.float32
    )
    in_coords = (
        in_coords.astype(jnp.bfloat16).reshape(examples_here, seq_slots, rank)
        * token_mask[:, :, None]
    )
    out_coords = jnp.dot(
        layer_grads.reshape(-1, width), proj_out[0].T, preferred_element_type=jnp.float32
    )
    out_coords = out_coords.astype(jnp.bfloat16).reshape(examples_here, seq_slots, rank)
    projected = jnp.einsum(
        "esj,esk->ejk", out_coords, in_coords, preferred_element_type=jnp.float32
    )
    projected = projected.astype(jnp.bfloat16).reshape(examples_here, rank * rank)
    norm_factor = 1.0 / (rank * (seq_slots * lax.axis_size("section")) ** 0.5)
    all_grads = lax.all_gather(projected, "dp", axis=0, tiled=True)
    partial_scores = jnp.dot(all_grads, queries[0].T, preferred_element_type=jnp.float32)
    layer_scores = lax.psum(partial_scores, "section")
    summed_scores = lax.all_to_all(layer_scores, "dp", split_axis=0, concat_axis=1, tiled=True)
    return summed_scores * norm_factor


def solution(mesh):
    placed = (
        P("section", "dp", None, None),
        P("section", "dp", None, None),
        P("section", None, None),
        P("section", None, None),
        P("section", "dp", None),
        P("dp", None),
    )
    return jax.shard_map(body, mesh=mesh, in_specs=placed, out_specs=P("dp", None), check_vma=False)
```

profile of v0, /device:TPU:2, one launch (start us, length us, event | category | flops | bytes accessed | tf_op | source)
XLA Modules:
  0.0 111.7 jit_solution(17932882797118903231)
XLA Ops:
  0.0 0.0 copy-start
  0.0 0.0 copy-start.1
  0.0 0.9 fusion.7
  0.9 0.4 copy-done
  1.2 3.6 %convolution_convert_fusion.1 = bf16[256,64]{0,1:T(8,128)(2,1)S(1)} fusion(bf16[256,8192]{1,0:T(8,128)(2,1)} %bitcast.21, bf16[1,64,8192]{2,1,0:T(8,128)(2,1)S(1)} %copy-done), kind=kOutput, calls=%fused_computation.1 | convolution fusion | flops 268451840 | bytes 5275648 | tf_op jit(solution)/shard_map/dot_general | solution.py:17
  4.8 0.0 copy-start.2
  4.8 0.1 copy.22
  4.9 0.0 copy-done.1
  5.0 3.6 %convolution_convert_fusion.2 = bf16[256,64]{0,1:T(8,128)(2,1)S(1)} fusion(bf16[256,8192]{1,0:T(8,128)(2,1)} %bitcast.22, bf16[1,64,8192]{2,1,0:T(8,128)(2,1)S(1)} %copy-done.1), kind=kOutput, calls=%fused_computation.2 | convolution fusion | flops 268451840 | bytes 5275648 | tf_op jit(solution)/shard_map/dot_general | solution.py:24
  8.5 0.1 reshape.39
  8.7 0.2 convolution_convert_fusion
  8.9 0.1 reshape.42
  9.0 24.9 %all-gather = bf16[16,4,4096]{2,1,0:T(4,128)(2,1)S(1)} all-gather(bf16[1,4,4096]{2,1,0:T(4,128)(2,1)S(1)} %reshape.42), channel_id=1, replica_groups=mesh['section'=16,'dp'=16] {'dp'}, dimensions={0}, use_global_device_ids=true | all-gather | bytes 557056 | tf_op jit(solution)/shard_map/all_gather | solution.py:33
  33.9 0.1 reshape.43
  34.1 0.0 copy-done.2
  34.1 0.3 fusion.2
  34.4 66.5 %psum.7 = f32[16,4,16]{2,1,0:T(4,128)S(1)} all-reduce(f32[16,4,16]{2,1,0:T(4,128)S(1)} %bitcast.23), channel_id=1, replica_groups=mesh['section'=16,'dp'=16] {'section'}, use_global_device_ids=true, to_apply=%region_0.0 | all-reduce | flops 1024 | bytes 8192 | tf_op jit(solution)/shard_map/psum | solution.py:35
  100.8 10.1 %all_to_all.13 = f32[16,4,16]{2,1,0:T(4,128)S(1)} all-to-all(f32[16,4,16]{2,1,0:T(4,128)S(1)} %psum.7), channel_id=1, replica_groups=mesh['section'=16,'dp'=16] {'dp'}, dimensions={0} | all-to-all | bytes 8192 | tf_op jit(solution)/shard_map/all_to_all | solution.py:36
  111.0 0.7 mul.25
  (2 shorter events, 0.0 us)
Async XLA Ops:
  0.0 1.2 %copy-start = (bf16[1,64,8192]{2,1,0:T(8,128)(2,1)S(1)}, bf16[1,64,8192]{2,1,0:T(8,128)(2,1)}, u32[]{:S(2)}) copy-start(bf16[1,64,8192]{2,1,0:T(8,128)(2,1)} %param.8) | copy-start | bytes 3145732
  0.0 4.9 %copy-start.1 = (bf16[1,64,8192]{2,1,0:T(8,128)(2,1)S(1)}, bf16[1,64,8192]{2,1,0:T(8,128)(2,1)}, u32[]{:S(2)}) copy-start(bf16[1,64,8192]{2,1,0:T(8,128)(2,1)} %param.9) | copy-start | bytes 3145732
  4.8 29.3 %copy-start.2 = (bf16[1,16,4096]{2,1,0:T(8,128)(2,1)S(1)}, bf16[1,16,4096]{2,1,0:T(8,128)(2,1)}, u32[]{:S(2)}) copy-start(bf16[1,16,4096]{2,1,0:T(8,128)(2,1)} %param.10) | copy-start | bytes 393220
where the time goes:
time: 114 us; the launch traced here: 112 us
  blocking collectives  102 us (89%)
  matrix products  7.66 us (7%)
  local copies, waits for them, and re-layouts  1.51 us (1%)
    psum x1, blocking collectives, body(): layer_scores = lax.psum(partial_scores, 'section')  66.5 us
    all_gather x1, blocking collectives, body(): all_grads = lax.all_gather(projected, 'dp', axis=0, tiled=True)  24.9 us
    all_to_all x1, blocking collectives, body(): lax.all_to_all(layer_scores, 'dp', split_axis=0, concat_axis=1, tiled=True)  10.1 us
    dot_general x1, matrix products, body(): jnp.dot(layer_grads.reshape(-1, width), proj_out[0].T, preferred_element_...  3.58 us
    dot_general x1, matrix products, body(): jnp.dot(layer_acts.reshape(-1, width), proj_in[0].T, preferred_element_ty...  3.58 us

commit v1 on v0

v1 whole, which is shorter than its diff:
```python
import functools

import jax
import jax.numpy as jnp
from jax import lax
from jax.experimental import pallas as pl
from jax.experimental.pallas import tpu as pltpu
from jax.sharding import Mesh, PartitionSpec as P

SECTION = ("xl", "z")
GROUP = ("xh", "y", "c")


def project_kernel(lengths_ref, acts_ref, grads_ref, in_ref, out_ref, projected_ref):
    examples, slots, width = acts_ref.shape[1:]
    rank = in_ref.shape[1]
    rows = examples * slots
    contract = (((1,), (1,)), ((), ()))
    in_coords = lax.dot_general(
        acts_ref[0].reshape(rows, width), in_ref[0], contract, preferred_element_type=jnp.float32
    )
    out_coords = lax.dot_general(
        grads_ref[0].reshape(rows, width), out_ref[0], contract, preferred_element_type=jnp.float32
    )
    out_coords = out_coords.astype(jnp.bfloat16)
    slot = lax.broadcasted_iota(jnp.int32, (slots, rank), 0)
    for e in range(examples):
        block = in_coords[e * slots:(e + 1) * slots]
        block = jnp.where(slot < lengths_ref[0, e], block, 0.0).astype(jnp.bfloat16)
        projected_ref[e] = lax.dot_general(
            out_coords[e * slots:(e + 1) * slots], block, (((0,), (0,)), ((), ())),
            preferred_element_type=jnp.float32,
        ).astype(jnp.bfloat16)


def project(activations, out_grads, proj_in, proj_out, lengths):
    examples, slots, width = activations.shape[1:]
    rank = proj_in.shape[1]
    whole = pl.BlockSpec(memory_space=pltpu.VMEM)
    return pl.pallas_call(
        project_kernel,
        out_shape=jax.ShapeDtypeStruct((examples, rank, rank), jnp.bfloat16),
        in_specs=[pl.BlockSpec(memory_space=pltpu.SMEM)] + [whole] * 4,
        out_specs=whole,
        compiler_params=pltpu.CompilerParams(vmem_limit_bytes=16 * 1024 * 1024),
        cost_estimate=pl.CostEstimate(
            flops=4 * examples * slots * width * rank, bytes_accessed=10 * 1024 * 1024, transcendentals=0
        ),
        name="project",
    )(lengths, activations, out_grads, proj_in, proj_out)


def swap(x, axis):
    return lax.ppermute(x, axis, [(0, 1), (1, 0)])


def body(activations, out_grads, proj_in, proj_out, queries, lengths):
    rank = proj_in.shape[1]
    slots = activations.shape[2]
    rows_y = lax.axis_size("y")
    own = queries[0]
    with jax.named_scope("queries_y"):
        along = lax.all_to_all(jnp.broadcast_to(own[None], (rows_y,) + own.shape), "y", 0, 0, tiled=True)
    with jax.named_scope("queries_core"):
        other = swap(along, "c")
    first = lax.axis_index("c") == 0
    stored = jnp.where(first, jnp.stack([along, other], 1), jnp.stack([other, along], 1))
    stored = stored.reshape(-1, own.shape[-1])
    with jax.named_scope("project"):
        projected = project(activations, out_grads, proj_in, proj_out, lengths).reshape(-1, rank * rank)
    with jax.named_scope("projected_xh"):
        distant = swap(projected, "xh")
    low = lax.axis_index("xh") == 0
    pair = jnp.where(low, jnp.concatenate([projected, distant]), jnp.concatenate([distant, projected]))
    partial = lax.dot_general(pair, stored, (((1,), (1,)), ((), ())), preferred_element_type=jnp.float32)
    partial = partial.reshape(2, 1, projected.shape[0], stored.shape[0])
    sections = lax.axis_size(SECTION)
    spread = jnp.broadcast_to(partial, (2, sections) + partial.shape[2:]).reshape((2 * sections,) + partial.shape[2:])
    with jax.named_scope("scores_all"):
        arrived = lax.all_to_all(spread, ("xh",) + SECTION, 0, 0, tiled=True)
    arrived = arrived.reshape((2, sections) + partial.shape[2:])
    summed = arrived.sum(1)
    norm_factor = 1.0 / (rank * (slots * sections) ** 0.5)
    return jnp.concatenate([summed[0], summed[1]], axis=1) * norm_factor


def solution(mesh):
    fine = Mesh(mesh.devices.reshape(2, 8, 2, 4, 2), SECTION + GROUP)
    placed = (
        P(SECTION, GROUP, None, None),
        P(SECTION, GROUP, None, None),
        P(SECTION, None, None),
        P(SECTION, None, None),
        P(SECTION, GROUP, None),
        P(GROUP, None),
    )
    return jax.shard_map(body, mesh=fine, in_specs=placed, out_specs=P(GROUP, None), check_vma=False)
```

time: 114 us -> 52.7 us (0.46); the launches traced: 112 us -> 52.3 us
  blocking collectives: 102 us -> 34 us
  matrix products: 7.66 us -> 0.39 us
  local copies, waits for them, and re-layouts: 1.51 us -> 8.6 us
  waiting for transfers between devices: 0 us -> 3.29 us
  Pallas kernels: 0 us -> 3.01 us
  starting transfers between devices: 0 us -> 2.22 us
    psum x1 -> x0, blocking collectives: 66.5 us -> none  [body(): layer_scores = lax.psum(partial_scores, 'section')]
    all_gather x1 -> x0, blocking collectives: 24.9 us -> none  [body(): all_grads = lax.all_gather(projected, 'dp', axis=0, tiled=True)]
    all_to_all x1 -> x2, blocking collectives: 10.1 us -> 34 us  [the longest x1 20.3 us: body(): arrived = lax.all_to_all(spread, ('xh',) + SECTION, 0, 0, tiled=True)]
    dot_general x4 -> x1, matrix products: 7.66 us -> 0.39 us  [body(): lax.dot_general(pair, stored, (((1,), (1,)), ((), ())), preferred_element...]
    unnamed x8 -> x10, local copies, waits for them, and re-layouts: 0.61 us -> 7.48 us
    ppermute x0 -> x2, waiting for transfers between devices: none -> 3.29 us  [swap(): return lax.ppermute(x, axis, [(0, 1), (1, 0)])]
    pallas_call x0 -> x1, Pallas kernels: none -> 3.01 us  [project(): pl.pallas_call(project_kernel, out_shape=jax.ShapeDtypeStruct((examples,...]
    ppermute x0 -> x2, starting transfers between devices: none -> 2.22 us  [swap(): return lax.ppermute(x, axis, [(0, 1), (1, 0)])]
  transfers between devices with their start and end apart: 0 -> 2, of which waited for: 0 -> 1; matrix products, arithmetic and copies ran while one was open for 0% -> 0% of each run, Pallas kernels for 0% -> 6%
where the time goes in v1:
time: 52.7 us; the launch traced here: 52.3 us
  blocking collectives  34 us (65%)
  local copies, waits for them, and re-layouts  8.6 us (16%)
  waiting for transfers between devices  3.29 us (6%)
  Pallas kernels  3.01 us (6%)
  starting transfers between devices  2.22 us (4%)
  other arithmetic  0.78 us (1%)
    all_to_all x1, blocking collectives, body(): arrived = lax.all_to_all(spread, ('xh',) + SECTION, 0, 0, tiled=True)  20.3 us
    all_to_all x1, blocking collectives, body(): lax.all_to_all(jnp.broadcast_to(own[None], (rows_y,) + own.shape), 'y', 0...  13.7 us
    unnamed x10, local copies, waits for them, and re-layouts  7.48 us
    ppermute x2, waiting for transfers between devices, swap(): return lax.ppermute(x, axis, [(0, 1), (1, 0)])  3.29 us
    pallas_call x1, Pallas kernels, project(): pl.pallas_call(project_kernel, out_shape=jax.ShapeDtypeStruct((examples,...  3.01 us
    ppermute x2, starting transfers between devices, swap(): return lax.ppermute(x, axis, [(0, 1), (1, 0)])  2.22 us
  transfers between devices with their start and end apart: 2, of which 1 were waited for; matrix products, arithmetic and copies ran while one was open for 0% of the time, Pallas kernels for 6%

profile of v1, /device:TPU:2, one launch (start us, length us, event | category | flops | bytes accessed | tf_op | source)
XLA Modules:
  0.0 52.3 jit_solution(8085419657624652747)
XLA Ops:
  0.0 0.9 %broadcast_in_dim.13 = bf16[4,16,4096]{2,1,0:T(8,128)(2,1)S(1)} broadcast(bf16[16,4096]{1,0:T(8,128)(2,1)} %bitcast.19), dimensions={1,2} | broadcast | bytes 655360 | tf_op jit(solution)/shard_map/queries_y/broadcast_in_dim | solution.py:63
  0.9 13.7 %all_to_all.10 = bf16[4,16,4096]{2,1,0:T(8,128)(2,1)S(1)} all-to-all(bf16[4,16,4096]{2,1,0:T(8,128)(2,1)S(1)} %broadcast_in_dim.13), channel_id=1, replica_groups=mesh['xl'=2,'z'=8,'xh'=2,'y'=4,'c'=2] {'y'}, dimensions={0} | all-to-all | bytes 1048576 | tf_op jit(solution)/shard_map/queries_y/all_to_all | solution.py:63
  14.7 0.0 collective-permute-start.1
  14.7 0.0 copy-start
  14.7 2.2 %copy-done = bf16[1,4,64,8192]{3,2,1,0:T(8,128)(2,1)S(1)} copy-done((bf16[1,4,64,8192]{3,2,1,0:T(8,128)(2,1)S(1)}, bf16[1,4,64,8192]{3,2,1,0:T(8,128)(2,1)}, u32[]{:S(2)}) %copy-start) | copy-done | bytes 4194328
  16.9 0.0 copy-start.1
  16.9 2.2 %copy-done.1 = bf16[1,4,64,8192]{3,2,1,0:T(8,128)(2,1)S(1)} copy-done((bf16[1,4,64,8192]{3,2,1,0:T(8,128)(2,1)S(1)}, bf16[1,4,64,8192]{3,2,1,0:T(8,128)(2,1)}, u32[]{:S(2)}) %copy-start.1) | copy-done | bytes 4194328
  19.1 0.0 copy-start.2
  19.1 1.2 %copy-done.2 = bf16[1,64,8192]{2,1,0:T(8,128)(2,1)S(1)} copy-done((bf16[1,64,8192]{2,1,0:T(8,128)(2,1)S(1)}, bf16[1,64,8192]{2,1,0:T(8,128)(2,1)}, u32[]{:S(2)}) %copy-start.2) | copy-done | bytes 1048600
  20.3 0.0 copy-start.3
  20.3 1.2 %copy-done.3 = bf16[1,64,8192]{2,1,0:T(8,128)(2,1)S(1)} copy-done((bf16[1,64,8192]{2,1,0:T(8,128)(2,1)S(1)}, bf16[1,64,8192]{2,1,0:T(8,128)(2,1)}, u32[]{:S(2)}) %copy-start.3) | copy-done | bytes 1048600
  21.5 0.0 copy-start.4
  21.5 0.7 %copy-done.4 = s32[1,4]{1,0:T(1,128)S(1)} copy-done((s32[1,4]{1,0:T(1,128)S(1)}, s32[1,4]{1,0:T(1,128)}, u32[]{:S(2)}) %copy-start.4) | copy-done | bytes 40
  22.2 3.0 %project.1 = bf16[4,64,64]{2,1,0:T(8,128)(2,1)S(1)} custom-call(s32[1,4]{1,0:T(1,128)S(1)} %copy-done.4, bf16[1,4,64,8192]{3,2,1,0:T(8,128)(2,1)S(1)} %copy-done, bf16[1,4,64,8192]{3,2,1,0:T(8,128)(2,1)S(1)} %copy-done.1, bf16[1,64,8192]{2,1,0:T(8,128)(2,1)S(1)} %copy-done.2, bf16[1,64,8192]{2,1,0:T(8,128)(2,1)S(1)} %copy-done.3), custom_call_target="tpu_custom_call" | custom-call | flops 536870912 | bytes 10485760 | tf_op jit(solution)/shard_map/project/project/pallas_call | solution.py:40
  25.2 0.1 reshape.40
  25.3 2.2 %collective-permute-start = (bf16[4,4096]{1,0:T(4,128)(2,1)S(1)}, bf16[4,4096]{1,0:T(4,128)(2,1)S(1)}, u32[]{:S(2)}, u32[]{:S(2)}) collective-permute-start(bf16[4,4096]{1,0:T(4,128)(2,1)S(1)} %reshape.40), channel_id=1, source_target_pairs={{0,8},{8,0},{1,9},{9,1},{2,10},{10,2},{3,11},{11,3},{4,12},{12,4},... | collective-permute-start | bytes 98312 | tf_op jit(solution)/shard_map/projected_xh/ppermute | solution.py:54
  27.5 3.3 %collective-permute-done = bf16[4,4096]{1,0:T(4,128)(2,1)S(1)} collective-permute-done((bf16[4,4096]{1,0:T(4,128)(2,1)S(1)}, bf16[4,4096]{1,0:T(4,128)(2,1)S(1)}, u32[]{:S(2)}, u32[]{:S(2)}) %collective-permute-start) | collective-permute-done | bytes 32800 | tf_op jit(solution)/shard_map/projected_xh/ppermute | solution.py:54
  30.8 0.1 maximum_select_fusion.1
  30.9 0.0 collective-permute-done.1
  30.9 0.1 maximum_select_fusion
  31.0 0.4 fusion
  31.4 20.3 %all_to_all.11 = f32[32,4,128]{2,1,0:T(4,128)S(1)} all-to-all(f32[32,4,128]{2,1,0:T(4,128)S(1)} %bitcast.18), channel_id=1, replica_groups=mesh['xl'=2,'z'=8,'xh'=2,'y'=4,'c'=2] {'xh','xl','z'}, dimensions={0} | all-to-all | bytes 131072 | tf_op jit(solution)/shard_map/scores_all/all_to_all | solution.py:80
  51.7 0.6 %maximum_multiply_fusion = f32[4,256]{1,0:T(4,128)} fusion(f32[4,128]{1,0:T(4,128)S(1)} %get-tuple-element.6, f32[4,128]{1,0:T(4,128)S(1)} %get-tuple-element.5), kind=kLoop, calls=%fused_computation.3 | loop fusion | flops 2048 | bytes 8192 | tf_op jit(solution)/shard_map/mul | solution.py:84
  (4 shorter events, 0.1 us)
Async XLA Ops:
  14.7 16.2 %collective-permute-start.1 = (bf16[4,16,4096]{2,1,0:T(8,128)(2,1)S(1)}, bf16[4,16,4096]{2,1,0:T(8,128)(2,1)S(1)}, u32[]{:S(2)}, u32[]{:S(2)}) collective-permute-start(bf16[4,16,4096]{2,1,0:T(8,128)(2,1)S(1)} %all_to_all.10), channel_id=1, source_target_pairs={{0,1},{1,0},{2,3},{3,2},{4,5},{5,4},{6,7},{7,6},{8,9},{9,8},{10,11... | collective-permute-start | bytes 1572872 | tf_op jit(solution)/shard_map/queries_core/ppermute | solution.py:54
  14.7 2.2 %copy-start = (bf16[1,4,64,8192]{3,2,1,0:T(8,128)(2,1)S(1)}, bf16[1,4,64,8192]{3,2,1,0:T(8,128)(2,1)}, u32[]{:S(2)}) copy-start(bf16[1,4,64,8192]{3,2,1,0:T(8,128)(2,1)} %acts_ref.1) | copy-start | bytes 12582916
  16.9 2.2 %copy-start.1 = (bf16[1,4,64,8192]{3,2,1,0:T(8,128)(2,1)S(1)}, bf16[1,4,64,8192]{3,2,1,0:T(8,128)(2,1)}, u32[]{:S(2)}) copy-start(bf16[1,4,64,8192]{3,2,1,0:T(8,128)(2,1)} %grads_ref.1) | copy-start | bytes 12582916
  19.1 1.2 %copy-start.2 = (bf16[1,64,8192]{2,1,0:T(8,128)(2,1)S(1)}, bf16[1,64,8192]{2,1,0:T(8,128)(2,1)}, u32[]{:S(2)}) copy-start(bf16[1,64,8192]{2,1,0:T(8,128)(2,1)} %in_ref.1) | copy-start | bytes 3145732
  20.3 1.2 %copy-start.3 = (bf16[1,64,8192]{2,1,0:T(8,128)(2,1)S(1)}, bf16[1,64,8192]{2,1,0:T(8,128)(2,1)}, u32[]{:S(2)}) copy-start(bf16[1,64,8192]{2,1,0:T(8,128)(2,1)} %out_ref.1) | copy-start | bytes 3145732
  21.5 0.7 %copy-start.4 = (s32[1,4]{1,0:T(1,128)S(1)}, s32[1,4]{1,0:T(1,128)}, u32[]{:S(2)}) copy-start(s32[1,4]{1,0:T(1,128)} %lengths_ref.1) | copy-start | bytes 52
  25.3 5.5 %collective-permute-start = (bf16[4,4096]{1,0:T(4,128)(2,1)S(1)}, bf16[4,4096]{1,0:T(4,128)(2,1)S(1)}, u32[]{:S(2)}, u32[]{:S(2)}) collective-permute-start(bf16[4,4096]{1,0:T(4,128)(2,1)S(1)} %reshape.40), channel_id=1, source_target_pairs={{0,8},{8,0},{1,9},{9,1},{2,10},{10,2},{3,11},{11,3},{4,12},{12,4},... | collective-permute-start | bytes 98312 | tf_op jit(solution)/shard_map/projected_xh/ppermute | solution.py:54

commit v2 on v1

v2 whole, which is shorter than its diff:
```python
import functools

import jax
import jax.numpy as jnp
from jax import lax
from jax.experimental import pallas as pl
from jax.experimental.pallas import tpu as pltpu
from jax.sharding import Mesh, PartitionSpec as P

SECTION = ("xl", "z")
GROUP = ("xh", "y", "c")


KEPT = 192
STEPS = 4
AHEAD = 3


def project_kernel(
    lengths_hbm, acts_ref, grads_ref, in_ref, out_ref, projected_ref,
    lengths_ref, acts_buf, grads_buf, in_buf, out_buf, token_sem, weight_sem, lengths_sem,
):
    lengths_copy = pltpu.make_async_copy(lengths_hbm, lengths_ref, lengths_sem)
    lengths_copy.start()
    examples, slots, width = acts_ref.shape[1:]
    rank = in_ref.shape[1]
    part = width // STEPS
    sides = ((acts_ref, in_ref, acts_buf, in_buf), (grads_ref, out_ref, grads_buf, out_buf))
    steps = [(side, k) for k in range(STEPS) for side in range(2)]

    def weight_copy(index):
        side, k = steps[index]
        columns = pl.ds(k * part, part)
        return pltpu.make_async_copy(
            sides[side][1].at[0, :, columns], sides[side][3].at[:, columns], weight_sem.at[index % AHEAD]
        )

    def start(index):
        side, k = steps[index]
        columns = pl.ds(k * part, part)
        if index >= AHEAD:
            weight_copy(index).start()
        for e in range(examples):
            pltpu.make_async_copy(
                sides[side][0].at[0, e, pl.ds(0, padded[e]), columns],
                sides[side][2].at[pl.ds(starts[e], padded[e]), columns],
                token_sem.at[index % AHEAD],
            ).start()

    def wait(index):
        side, k = steps[index]
        weight_copy(index).wait()
        rows = sides[side][2].at[pl.ds(0, total), pl.ds(k * part, part)]
        pltpu.make_async_copy(rows, rows, token_sem.at[index % AHEAD]).wait()

    for index in range(AHEAD):
        weight_copy(index).start()
    lengths_copy.wait()
    used = [lengths_ref[0, e] for e in range(examples)]
    padded = [pl.multiple_of((u + 15) // 16 * 16, 16) for u in used]
    starts = [0]
    for e in range(examples):
        starts.append(pl.multiple_of(starts[e] + padded[e], 16))
    total = starts[examples]
    for index in range(AHEAD):
        start(index)
    coords = [None, None]
    for index, (side, k) in enumerate(steps):
        wait(index)
        if index + AHEAD < len(steps):
            start(index + AHEAD)
        columns = slice(k * part, (k + 1) * part)
        term = lax.dot_general(
            sides[side][2][:, columns], sides[side][3][:, columns], (((1,), (1,)), ((), ())),
            preferred_element_type=jnp.float32,
        )
        coords[side] = term if k == 0 else coords[side] + term
    row = lax.broadcasted_iota(jnp.int32, (KEPT, rank), 0)
    blocks = [
        jnp.where((row >= starts[e]) & (row < starts[e] + used[e]), coords[0], 0.0).astype(jnp.bfloat16)
        for e in range(examples)
    ]
    out_coords = jnp.where(row < total, coords[1], 0.0).astype(jnp.bfloat16)
    projected = lax.dot_general(
        out_coords, jnp.concatenate(blocks, axis=1), (((0,), (0,)), ((), ())),
        preferred_element_type=jnp.float32,
    ).astype(jnp.bfloat16)
    for e in range(examples):
        projected_ref[e] = projected[:, e * rank:(e + 1) * rank]


def project(activations, out_grads, proj_in, proj_out, lengths):
    examples, slots, width = activations.shape[1:]
    rank = proj_in.shape[1]
    far = pl.BlockSpec(memory_space=pltpu.HBM)
    kept = [pltpu.with_memory_space_constraint(x, pltpu.HBM) for x in (lengths, activations, out_grads, proj_in, proj_out)]
    return pl.pallas_call(
        project_kernel,
        out_shape=pltpu.VMEM((examples, rank, rank), jnp.bfloat16),
        in_specs=[far] * 5,
        out_specs=pl.BlockSpec(memory_space=pltpu.VMEM),
        scratch_shapes=[
            pltpu.SMEM(lengths.shape, jnp.int32),
            pltpu.VMEM((KEPT, width), jnp.bfloat16),
            pltpu.VMEM((KEPT, width), jnp.bfloat16),
            pltpu.VMEM((rank, width), jnp.bfloat16),
            pltpu.VMEM((rank, width), jnp.bfloat16),
            pltpu.SemaphoreType.DMA((AHEAD,)),
            pltpu.SemaphoreType.DMA((AHEAD,)),
            pltpu.SemaphoreType.DMA,
        ],
        compiler_params=pltpu.CompilerParams(vmem_limit_bytes=16 * 1024 * 1024),
        cost_estimate=pl.CostEstimate(
            flops=4 * KEPT * width * rank, bytes_accessed=16 * 1024 * 1024, transcendentals=0
        ),
        name="project",
    )(*kept)


def swap(x, axis):
    return lax.ppermute(x, axis, [(0, 1), (1, 0)])


def body(activations, out_grads, proj_in, proj_out, queries, lengths):
    rank = proj_in.shape[1]
    slots = activations.shape[2]
    rows_y = lax.axis_size("y")
    own = queries[0]
    with jax.named_scope("queries_y"):
        me = lax.axis_index("y")
        hops = [lax.ppermute(own, "y", [(i, (i + d) % rows_y) for i in range(rows_y)]) for d in range(1, rows_y)]
        from_back = jnp.stack([own] + hops)
        along = jnp.stack([lax.dynamic_index_in_dim(from_back, lax.rem(me - i + rows_y, rows_y), 0, False) for i in range(rows_y)])
    with jax.named_scope("project"):
        projected = project(activations, out_grads, proj_in, proj_out, lengths).reshape(-1, rank * rank)
    with jax.named_scope("projected_xh"):
        distant = swap(projected, "xh")
    along = along + projected[0, 0] * 0
    with jax.named_scope("queries_core"):
        other = swap(along, "c")
    first = lax.axis_index("c") == 0
    stored = jnp.where(first, jnp.stack([along, other], 1), jnp.stack([other, along], 1))
    stored = stored.reshape(-1, own.shape[-1])
    low = lax.axis_index("xh") == 0
    pair = jnp.where(low, jnp.concatenate([projected, distant]), jnp.concatenate([distant, projected]))
    partial = lax.dot_general(pair, stored, (((1,), (1,)), ((), ())), preferred_element_type=jnp.float32)
    partial = partial.reshape(2, 1, projected.shape[0], stored.shape[0])
    sections = lax.axis_size(SECTION)
    spread = jnp.broadcast_to(partial, (2, sections) + partial.shape[2:]).reshape((2 * sections,) + partial.shape[2:])
    with jax.named_scope("scores_all"):
        arrived = lax.all_to_all(spread, ("xh",) + SECTION, 0, 0, tiled=True)
    arrived = arrived.reshape((2, sections) + partial.shape[2:])
    summed = arrived.sum(1)
    norm_factor = 1.0 / (rank * (slots * sections) ** 0.5)
    return jnp.concatenate([summed[0], summed[1]], axis=1) * norm_factor


def solution(mesh):
    fine = Mesh(mesh.devices.reshape(2, 8, 2, 4, 2), SECTION + GROUP)
    placed = (
        P(SECTION, GROUP, None, None),
        P(SECTION, GROUP, None, None),
        P(SECTION, None, None),
        P(SECTION, None, None),
        P(SECTION, GROUP, None),
        P(GROUP, None),
    )
    return jax.shard_map(body, mesh=fine, in_specs=placed, out_specs=P(GROUP, None), check_vma=False)
```

time: 52.7 us -> 39.6 us (0.75)
  blocking collectives: 34 us -> 20.3 us
  local copies, waits for them, and re-layouts: 8.6 us -> 0.73 us
  starting transfers between devices: 2.22 us -> 8.14 us
  Pallas kernels: 3.01 us -> 6.28 us
  waiting for transfers between devices: 3.29 us -> 1.76 us
  between operations: 0.05 us -> 0.77 us
    all_to_all x1 -> x0, blocking collectives: 13.7 us -> none  [body(): lax.all_to_all(jnp.broadcast_to(own[None], (rows_y,) + own.shape), 'y', 0...]
    unnamed x10 -> x2, local copies, waits for them, and re-layouts: 7.48 us -> 0.01 us
    ppermute x0 -> x3, starting transfers between devices: none -> 5.83 us  [body(): lax.ppermute(own, 'y', [(i, (i + d) % rows_y) for i in range(rows_y)])]
    pallas_call x1, Pallas kernels: 3.01 us -> 6.28 us  [project(): pl.pallas_call(project_kernel, out_shape=pltpu.VMEM((examples, rank, rank...]
    ppermute x2, waiting for transfers between devices: 3.29 us -> 1.76 us  [swap(): return lax.ppermute(x, axis, [(0, 1), (1, 0)])]
    broadcast_in_dim x1 -> x0, local copies, waits for them, and re-layouts: 0.94 us -> none  [body(): jnp.broadcast_to(own[None], (rows_y,) + own.shape)]
  transfers between devices with their start and end apart: 2 -> 5, of which waited for: 1 -> 1; matrix products, arithmetic and copies ran while one was open for 0% -> 3% of each run, Pallas kernels for 6% -> 16%
where the time goes in v2:
time: 39.6 us; the launch traced here: 39.4 us
  blocking collectives  20.3 us (51%)
  starting transfers between devices  8.14 us (21%)
  Pallas kernels  6.28 us (16%)
  waiting for transfers between devices  1.76 us (4%)
  other arithmetic  1.02 us (3%)
  between operations  0.77 us (2%)
  local copies, waits for them, and re-layouts  0.73 us (2%)
    all_to_all x1, blocking collectives, body(): arrived = lax.all_to_all(spread, ('xh',) + SECTION, 0, 0, tiled=True)  20.3 us
    pallas_call x1, Pallas kernels, project(): pl.pallas_call(project_kernel, out_shape=pltpu.VMEM((examples, rank, rank...  6.28 us
    ppermute x3, starting transfers between devices, body(): lax.ppermute(own, 'y', [(i, (i + d) % rows_y) for i in range(rows_y)])  5.83 us
    ppermute x2, starting transfers between devices, swap(): return lax.ppermute(x, axis, [(0, 1), (1, 0)])  2.32 us
    ppermute x2, waiting for transfers between devices, swap(): return lax.ppermute(x, axis, [(0, 1), (1, 0)])  1.76 us
  transfers between devices with their start and end apart: 5, of which 1 were waited for; matrix products, arithmetic and copies ran while one was open for 3% of the time, Pallas kernels for 16%

profile of v2, /device:TPU:2, one launch (start us, length us, event | category | flops | bytes accessed | tf_op | source)
XLA Modules:
  0.0 39.4 jit_solution(9967341781048441488)
XLA Ops:
  0.0 0.0 copy-start
  0.0 1.6 %collective-permute-start.1 = (bf16[16,4096]{1,0:T(8,128)(2,1)}, bf16[16,4096]{1,0:T(8,128)(2,1)S(1)}, u32[]{:S(2)}, u32[]{:S(2)}) collective-permute-start(bf16[16,4096]{1,0:T(8,128)(2,1)} %bitcast.29), channel_id=1, source_target_pairs={{0,2},{2,4},{4,6},{6,0},{1,3},{3,5},{5,7},{7,1},{8,10},{10,12},{12... | collective-permute-start | bytes 393224 | tf_op jit(solution)/shard_map/queries_y/ppermute | solution.py:131
  1.6 2.9 %collective-permute-start.2 = (bf16[16,4096]{1,0:T(8,128)(2,1)}, bf16[16,4096]{1,0:T(8,128)(2,1)S(1)}, u32[]{:S(2)}, u32[]{:S(2)}) collective-permute-start(bf16[16,4096]{1,0:T(8,128)(2,1)} %bitcast.30), channel_id=1, source_target_pairs={{0,4},{2,6},{4,0},{6,2},{1,5},{3,7},{5,1},{7,3},{8,12},{10,14},{12... | collective-permute-start | bytes 393224 | tf_op jit(solution)/shard_map/queries_y/ppermute | solution.py:131
  4.5 1.3 %collective-permute-start.3 = (bf16[16,4096]{1,0:T(8,128)(2,1)}, bf16[16,4096]{1,0:T(8,128)(2,1)S(1)}, u32[]{:S(2)}, u32[]{:S(2)}) collective-permute-start(bf16[16,4096]{1,0:T(8,128)(2,1)} %bitcast.31), channel_id=1, source_target_pairs={{0,6},{2,0},{4,2},{6,4},{1,7},{3,1},{5,3},{7,5},{8,14},{10,8},{12,... | collective-permute-start | bytes 393224 | tf_op jit(solution)/shard_map/queries_y/ppermute | solution.py:131
  5.8 6.3 %project.1 = bf16[4,64,64]{2,1,0:T(8,128)(2,1)S(1)} custom-call(s32[1,4]{1,0:T(1,128)} %lengths_hbm.1, bf16[1,4,64,8192]{3,2,1,0:T(8,128)(2,1)} %acts_ref.1, bf16[1,4,64,8192]{3,2,1,0:T(8,128)(2,1)} %grads_ref.1, bf16[1,64,8192]{2,1,0:T(8,128)(2,1)} %in_ref.1, bf16[1,64,8192]{2,1,0:T(8,128)(2,1)} %out_ref.1), custom_call_target="tpu_custom_call" | custom-call | flops 402653184 | bytes 16777216 | tf_op jit(solution)/shard_map/project/project/pallas_call | solution.py:97
  12.1 0.1 reshape.97
  12.2 2.2 %collective-permute-start = (bf16[4,4096]{1,0:T(4,128)(2,1)S(1)}, bf16[4,4096]{1,0:T(4,128)(2,1)S(1)}, u32[]{:S(2)}, u32[]{:S(2)}) collective-permute-start(bf16[4,4096]{1,0:T(4,128)(2,1)S(1)} %reshape.97), channel_id=1, source_target_pairs={{0,8},{8,0},{1,9},{9,1},{2,10},{10,2},{3,11},{11,3},{4,12},{12,4},... | collective-permute-start | bytes 98312 | tf_op jit(solution)/shard_map/projected_xh/ppermute | solution.py:121
  14.5 0.5 %slice.12 = bf16[1,1]{1,0:T(2,128)(2,1)} slice(bf16[4,4096]{1,0:T(4,128)(2,1)S(1)} %reshape.97), slice={[0:1], [0:1]} | slice | bytes 4 | tf_op jit(solution)/shard_map/slice | solution.py:138
  15.6 0.0 collective-permute-done.1
  15.6 0.0 collective-permute-done.2
  15.6 0.0 collective-permute-done.3
  15.7 0.0 copy-done
  15.7 0.1 pad_maximum_fusion
  15.8 0.1 maximum_add_fusion.1
  15.9 0.1 collective-permute-start.4
  16.0 1.8 %collective-permute-done = bf16[4,4096]{1,0:T(4,128)(2,1)S(1)} collective-permute-done((bf16[4,4096]{1,0:T(4,128)(2,1)S(1)}, bf16[4,4096]{1,0:T(4,128)(2,1)S(1)}, u32[]{:S(2)}, u32[]{:S(2)}) %collective-permute-start) | collective-permute-done | bytes 32800 | tf_op jit(solution)/shard_map/projected_xh/ppermute | solution.py:121
  17.7 0.1 maximum_select_fusion.1
  17.8 0.1 maximum_add_fusion
  17.9 0.0 collective-permute-done.4
  17.9 0.1 maximum_select_fusion
  18.0 0.4 fusion
  18.5 20.3 %all_to_all.5 = f32[32,4,128]{2,1,0:T(4,128)S(1)} all-to-all(f32[32,4,128]{2,1,0:T(4,128)S(1)} %bitcast.28), channel_id=1, replica_groups=mesh['xl'=2,'z'=8,'xh'=2,'y'=4,'c'=2] {'xh','xl','z'}, dimensions={0} | all-to-all | bytes 131072 | tf_op jit(solution)/shard_map/scores_all/all_to_all | solution.py:151
  38.8 0.6 %maximum_multiply_fusion = f32[4,256]{1,0:T(4,128)} fusion(f32[4,128]{1,0:T(4,128)S(1)} %get-tuple-element.10, f32[4,128]{1,0:T(4,128)S(1)} %get-tuple-element.9), kind=kLoop, calls=%fused_computation.6 | loop fusion | flops 2048 | bytes 8192 | tf_op jit(solution)/shard_map/mul | solution.py:155
  (5 shorter events, 0.1 us)
Async XLA Ops:
  0.0 15.7 %copy-start = (bf16[1,16,4096]{2,1,0:T(8,128)(2,1)S(1)}, bf16[1,16,4096]{2,1,0:T(8,128)(2,1)}, u32[]{:S(2)}) copy-start(bf16[1,16,4096]{2,1,0:T(8,128)(2,1)} %param.10) | copy-start | bytes 393220
  0.0 15.6 %collective-permute-start.1 = (bf16[16,4096]{1,0:T(8,128)(2,1)}, bf16[16,4096]{1,0:T(8,128)(2,1)S(1)}, u32[]{:S(2)}, u32[]{:S(2)}) collective-permute-start(bf16[16,4096]{1,0:T(8,128)(2,1)} %bitcast.29), channel_id=1, source_target_pairs={{0,2},{2,4},{4,6},{6,0},{1,3},{3,5},{5,7},{7,1},{8,10},{10,12},{12... | collective-permute-start | bytes 393224 | tf_op jit(solution)/shard_map/queries_y/ppermute | solution.py:131
  1.6 14.1 %collective-permute-start.2 = (bf16[16,4096]{1,0:T(8,128)(2,1)}, bf16[16,4096]{1,0:T(8,128)(2,1)S(1)}, u32[]{:S(2)}, u32[]{:S(2)}) collective-permute-start(bf16[16,4096]{1,0:T(8,128)(2,1)} %bitcast.30), channel_id=1, source_target_pairs={{0,4},{2,6},{4,0},{6,2},{1,5},{3,7},{5,1},{7,3},{8,12},{10,14},{12... | collective-permute-start | bytes 393224 | tf_op jit(solution)/shard_map/queries_y/ppermute | solution.py:131
  4.5 11.2 %collective-permute-start.3 = (bf16[16,4096]{1,0:T(8,128)(2,1)}, bf16[16,4096]{1,0:T(8,128)(2,1)S(1)}, u32[]{:S(2)}, u32[]{:S(2)}) collective-permute-start(bf16[16,4096]{1,0:T(8,128)(2,1)} %bitcast.31), channel_id=1, source_target_pairs={{0,6},{2,0},{4,2},{6,4},{1,7},{3,1},{5,3},{7,5},{8,14},{10,8},{12,... | collective-permute-start | bytes 393224 | tf_op jit(solution)/shard_map/queries_y/ppermute | solution.py:131
  12.2 5.5 %collective-permute-start = (bf16[4,4096]{1,0:T(4,128)(2,1)S(1)}, bf16[4,4096]{1,0:T(4,128)(2,1)S(1)}, u32[]{:S(2)}, u32[]{:S(2)}) collective-permute-start(bf16[4,4096]{1,0:T(4,128)(2,1)S(1)} %reshape.97), channel_id=1, source_target_pairs={{0,8},{8,0},{1,9},{9,1},{2,10},{10,2},{3,11},{11,3},{4,12},{12,4},... | collective-permute-start | bytes 98312 | tf_op jit(solution)/shard_map/projected_xh/ppermute | solution.py:121
  15.9 2.0 %collective-permute-start.4 = (bf16[4,16,4096]{2,1,0:T(8,128)(2,1)S(1)}, bf16[4,16,4096]{2,1,0:T(8,128)(2,1)S(1)}, u32[]{:S(2)}, u32[]{:S(2)}) collective-permute-start(bf16[4,16,4096]{2,1,0:T(8,128)(2,1)S(1)} %maximum_add_fusion.1), channel_id=1, source_target_pairs={{0,1},{1,0},{2,3},{3,2},{4,5},{5,4},{6,7},{7,6},{8,9},{9,8},{10,11... | collective-permute-start | bytes 1572872 | tf_op jit(solution)/shard_map/queries_core/ppermute | solution.py:121

commit v3 on v1

v3 whole, which is shorter than its diff:
```python
import jax
import jax.numpy as jnp
from jax import lax
from jax.experimental import pallas as pl
from jax.experimental.pallas import tpu as pltpu
from jax.sharding import Mesh, PartitionSpec as P

SECTION = ("xl", "z")
GROUP = ("xh", "y", "c")
FINAL = ("xh", "xl", "z")
STEPS = 8
AHEAD = 4
ORDER = (1, 2, 3)
BOTH_LAST = (((1,), (1,)), ((), ()))
BOTH_FIRST = (((0,), (0,)), ((), ()))


def project_kernel(
    lengths_hbm, acts_ref, grads_ref, in_ref, out_ref, projected_ref,
    lengths_ref, acts_buf, grads_buf, in_buf, out_buf, sums_ref, piece_sem, lengths_sem,
):
    rank, width = in_ref.shape
    examples = projected_ref.shape[0]
    slots = acts_ref.shape[0] // examples
    part = width // STEPS
    pairs = ((in_ref, in_buf), (acts_ref, acts_buf), (out_ref, out_buf), (grads_ref, grads_buf))

    def copies(k, slot):
        columns = pl.ds(pl.multiple_of(k * part, part), part)
        return [
            pltpu.make_async_copy(source.at[:, columns], target.at[:, columns], piece_sem.at[i, slot])
            for i, (source, target) in enumerate(pairs)
        ]

    lengths_copy = pltpu.make_async_copy(lengths_hbm, lengths_ref, lengths_sem)
    lengths_copy.start()
    for k in range(AHEAD):
        for copy in copies(k, k):
            copy.start()
    sums_ref[...] = jnp.zeros_like(sums_ref)

    def step(k, carry):
        slot = lax.rem(k, AHEAD)
        for copy in copies(k, slot):
            copy.wait()

        @pl.when(k + AHEAD < STEPS)
        def _():
            for copy in copies(k + AHEAD, slot):
                copy.start()

        columns = pl.ds(pl.multiple_of(k * part, part), part)
        sums_ref[0] += lax.dot_general(
            acts_buf[:, columns], in_buf[:, columns], BOTH_LAST, preferred_element_type=jnp.float32
        )
        sums_ref[1] += lax.dot_general(
            grads_buf[:, columns], out_buf[:, columns], BOTH_LAST, preferred_element_type=jnp.float32
        )
        return carry

    lax.fori_loop(0, STEPS, step, 0)
    lengths_copy.wait()
    slot = lax.broadcasted_iota(jnp.int32, (slots, rank), 0)
    for e in range(examples):
        rows = slice(e * slots, (e + 1) * slots)
        in_coords = jnp.where(slot < lengths_ref[0, e], sums_ref[0, rows], 0.0).astype(jnp.bfloat16)
        out_coords = sums_ref[1, rows].astype(jnp.bfloat16)
        projected_ref[e] = lax.dot_general(
            out_coords, in_coords, BOTH_FIRST, preferred_element_type=jnp.float32
        ).astype(jnp.bfloat16)


def project(activations, out_grads, proj_in, proj_out, lengths):
    examples, slots, width = activations.shape[1:]
    rank = proj_in.shape[1]
    rows = examples * slots
    far = pl.BlockSpec(memory_space=pltpu.HBM)
    operands = (lengths, activations.reshape(rows, width), out_grads.reshape(rows, width), proj_in[0], proj_out[0])
    return pl.pallas_call(
        project_kernel,
        out_shape=pltpu.VMEM((examples, rank, rank), jnp.bfloat16),
        in_specs=[far] * len(operands),
        out_specs=pl.BlockSpec(memory_space=pltpu.VMEM),
        scratch_shapes=[
            pltpu.SMEM(lengths.shape, jnp.int32),
            pltpu.VMEM((rows, width), jnp.bfloat16),
            pltpu.VMEM((rows, width), jnp.bfloat16),
            pltpu.VMEM((rank, width), jnp.bfloat16),
            pltpu.VMEM((rank, width), jnp.bfloat16),
            pltpu.VMEM((2, rows, rank), jnp.float32),
            pltpu.SemaphoreType.DMA((4, AHEAD)),
            pltpu.SemaphoreType.DMA,
        ],
        compiler_params=pltpu.CompilerParams(vmem_limit_bytes=16 * 1024 * 1024),
        cost_estimate=pl.CostEstimate(
            flops=4 * rows * width * rank, bytes_accessed=16 * 1024 * 1024, transcendentals=0
        ),
        name="project",
    )(*[pltpu.with_memory_space_constraint(x, pltpu.HBM) for x in operands])


def exchange(x, axis, distance):
    return lax.ppermute(x, axis, [(i, i ^ distance) for i in range(lax.axis_size(axis))])


def body(activations, out_grads, proj_in, proj_out, queries, lengths):
    rank = proj_in.shape[1]
    slots = activations.shape[2]
    own = queries[0]
    with jax.named_scope("queries_y"):
        me = lax.axis_index("y")
        held = {0: own}
        for distance in ORDER:
            held[distance] = exchange(own, "y", distance)
    with jax.named_scope("project"):
        projected = project(activations, out_grads, proj_in, proj_out, lengths).reshape(-1, rank * rank)
    with jax.named_scope("projected_xh"):
        distant = exchange(projected, "xh", 1)
    by_distance = jnp.stack([held[d] for d in range(len(held))])
    along = jnp.stack([lax.dynamic_index_in_dim(by_distance, me ^ i, 0, False) for i in range(len(held))])
    along = along + projected[0, 0] * 0
    with jax.named_scope("queries_core"):
        other = exchange(along, "c", 1)
    first = lax.axis_index("c") == 0
    stored = jnp.where(first, jnp.stack([along, other], 1), jnp.stack([other, along], 1))
    stored = stored.reshape(-1, own.shape[-1])
    low = lax.axis_index("xh") == 0
    pair = jnp.where(low, jnp.concatenate([projected, distant]), jnp.concatenate([distant, projected]))
    partial = lax.dot_general(pair, stored, BOTH_LAST, preferred_element_type=jnp.float32)
    sections = lax.axis_size(SECTION)
    sizes = [lax.axis_size(axis) for axis in FINAL]
    at = FINAL.index("xh")
    partial = partial.reshape([2 if i == at else 1 for i in range(3)] + [projected.shape[0], -1])
    spread = jnp.broadcast_to(partial, tuple(sizes) + partial.shape[3:]).reshape((-1,) + partial.shape[3:])
    with jax.named_scope("scores_all"):
        arrived = lax.all_to_all(spread, FINAL, 0, 0, tiled=True)
    arrived = arrived.reshape(tuple(sizes) + arrived.shape[1:])
    summed = arrived.sum([i for i in range(3) if i != at])
    norm_factor = 1.0 / (rank * (slots * sections) ** 0.5)
    return jnp.concatenate([summed[0], summed[1]], axis=1) * norm_factor


def solution(mesh):
    fine = Mesh(mesh.devices.reshape(2, 8, 2, 4, 2), SECTION + GROUP)
    placed = (
        P(SECTION, GROUP, None, None),
        P(SECTION, GROUP, None, None),
        P(SECTION, None, None),
        P(SECTION, None, None),
        P(SECTION, GROUP, None),
        P(GROUP, None),
    )
    return jax.shard_map(body, mesh=fine, in_specs=placed, out_specs=P(GROUP, None), check_vma=False)
```

time: 52.7 us -> 38.2 us (0.72)
  the two profiles are of different devices: /device:TPU:2 before, /device:TPU:24 now
where the time goes in v3:
time: 38.2 us; the launch traced here: 38.1 us
  blocking collectives  20.4 us (53%)
  starting transfers between devices  7.9 us (21%)
  Pallas kernels  5.21 us (14%)
  waiting for transfers between devices  1.72 us (5%)
  other arithmetic  1.02 us (3%)
  between operations  0.77 us (2%)
  local copies, waits for them, and re-layouts  0.73 us (2%)
  matrix products  0.39 us (1%)
    all_to_all x1, blocking collectives, body(): arrived = lax.all_to_all(spread, FINAL, 0, 0, tiled=True)  20.4 us
    ppermute x5, starting transfers between devices, exchange(): lax.ppermute(x, axis, [(i, i ^ distance) for i in range(lax.axis_size(axi...  7.9 us
    pallas_call x1, Pallas kernels, project(): pl.pallas_call(project_kernel, out_shape=pltpu.VMEM((examples, rank, rank...  5.21 us
    ppermute x5, waiting for transfers between devices, exchange(): lax.ppermute(x, axis, [(i, i ^ distance) for i in range(lax.axis_size(axi...  1.72 us
  transfers between devices with their start and end apart: 5, of which 2 were waited for; matrix products, arithmetic and copies ran while one was open for 3% of the time, Pallas kernels for 14%

profile of v3, /device:TPU:24, one launch (start us, length us, event | category | flops | bytes accessed | tf_op | source)
XLA Modules:
  0.0 38.1 jit_solution(12633870033009246743)
XLA Ops:
  0.0 0.7 %collective-permute-start.1 = (bf16[16,4096]{1,0:T(8,128)(2,1)}, bf16[16,4096]{1,0:T(8,128)(2,1)S(1)}, u32[]{:S(2)}, u32[]{:S(2)}) collective-permute-start(bf16[16,4096]{1,0:T(8,128)(2,1)} %bitcast.37), channel_id=1, source_target_pairs={{0,2},{2,0},{4,6},{6,4},{1,3},{3,1},{5,7},{7,5},{8,10},{10,8},{12,... | collective-permute-start | bytes 393224 | tf_op jit(solution)/shard_map/queries_y/ppermute | solution.py:103
  0.7 2.7 %collective-permute-start.2 = (bf16[16,4096]{1,0:T(8,128)(2,1)}, bf16[16,4096]{1,0:T(8,128)(2,1)S(1)}, u32[]{:S(2)}, u32[]{:S(2)}) collective-permute-start(bf16[16,4096]{1,0:T(8,128)(2,1)} %bitcast.38), channel_id=1, source_target_pairs={{0,4},{2,6},{4,0},{6,2},{1,5},{3,7},{5,1},{7,3},{8,12},{10,14},{12... | collective-permute-start | bytes 393224 | tf_op jit(solution)/shard_map/queries_y/ppermute | solution.py:103
  3.4 1.3 %collective-permute-start.3 = (bf16[16,4096]{1,0:T(8,128)(2,1)}, bf16[16,4096]{1,0:T(8,128)(2,1)S(1)}, u32[]{:S(2)}, u32[]{:S(2)}) collective-permute-start(bf16[16,4096]{1,0:T(8,128)(2,1)} %bitcast.39), channel_id=1, source_target_pairs={{0,6},{2,4},{4,2},{6,0},{1,7},{3,5},{5,3},{7,1},{8,14},{10,12},{12... | collective-permute-start | bytes 393224 | tf_op jit(solution)/shard_map/queries_y/ppermute | solution.py:103
  4.7 0.0 copy-start
  4.7 5.2 %project.1 = bf16[4,64,64]{2,1,0:T(8,128)(2,1)S(1)} custom-call(s32[1,4]{1,0:T(1,128)} %lengths_hbm.1, bf16[256,8192]{1,0:T(8,128)(2,1)} %bitcast.27, bf16[256,8192]{1,0:T(8,128)(2,1)} %bitcast.28, bf16[64,8192]{1,0:T(8,128)(2,1)} %bitcast.33, bf16[64,8192]{1,0:T(8,128)(2,1)} %bitcast.34), custom_call_target="tpu_custom_call" | custom-call | flops 536870912 | bytes 16777216 | tf_op jit(solution)/shard_map/project/project/pallas_call | solution.py:79
  9.9 0.1 reshape.105
  10.0 3.1 %collective-permute-start = (bf16[4,4096]{1,0:T(4,128)(2,1)S(1)}, bf16[4,4096]{1,0:T(4,128)(2,1)S(1)}, u32[]{:S(2)}, u32[]{:S(2)}) collective-permute-start(bf16[4,4096]{1,0:T(4,128)(2,1)S(1)} %reshape.105), channel_id=1, source_target_pairs={{0,8},{8,0},{1,9},{9,1},{2,10},{10,2},{3,11},{11,3},{4,12},{12,4},... | collective-permute-start | bytes 98312 | tf_op jit(solution)/shard_map/projected_xh/ppermute | solution.py:103
  13.1 0.5 %slice.12 = bf16[1,1]{1,0:T(2,128)(2,1)} slice(bf16[4,4096]{1,0:T(4,128)(2,1)S(1)} %reshape.105), slice={[0:1], [0:1]} | slice | bytes 4 | tf_op jit(solution)/shard_map/slice | solution.py:121
  14.3 0.0 collective-permute-done.1
  14.3 0.0 collective-permute-done.2
  14.3 0.0 collective-permute-done.3
  14.3 0.0 copy-done
  14.4 0.1 pad_maximum_fusion
  14.5 0.1 maximum_add_fusion.1
  14.6 0.1 collective-permute-start.4
  14.7 0.9 %collective-permute-done = bf16[4,4096]{1,0:T(4,128)(2,1)S(1)} collective-permute-done((bf16[4,4096]{1,0:T(4,128)(2,1)S(1)}, bf16[4,4096]{1,0:T(4,128)(2,1)S(1)}, u32[]{:S(2)}, u32[]{:S(2)}) %collective-permute-start) | collective-permute-done | bytes 32800 | tf_op jit(solution)/shard_map/projected_xh/ppermute | solution.py:103
  15.5 0.1 maximum_select_fusion.1
  15.6 0.1 maximum_add_fusion
  15.7 0.8 %collective-permute-done.4 = bf16[4,16,4096]{2,1,0:T(8,128)(2,1)S(1)} collective-permute-done((bf16[4,16,4096]{2,1,0:T(8,128)(2,1)S(1)}, bf16[4,16,4096]{2,1,0:T(8,128)(2,1)S(1)}, u32[]{:S(2)}, u32[]{:S(2)}) %collective-permute-start.4) | collective-permute-done | bytes 524320 | tf_op jit(solution)/shard_map/queries_core/ppermute | solution.py:103
  16.6 0.1 maximum_select_fusion
  16.7 0.4 %fusion = f32[2,4,128]{2,1,0:T(4,128)S(1)} fusion(bf16[2,4,4096]{2,1,0:T(4,128)(2,1)S(1)} %select_n.51, bf16[128,4096,1]{1,0,2:T(8,128)(2,1)S(1)} %bitcast.26), kind=kOutput, calls=%fused_computation.13 | convolution fusion | flops 8388608 | bytes 1118208 | tf_op jit(solution)/shard_map/dot_general | solution.py:129
  17.1 20.4 %all_to_all.5 = f32[32,4,128]{2,1,0:T(4,128)S(1)} all-to-all(f32[32,4,128]{2,1,0:T(4,128)S(1)} %bitcast.36), channel_id=1, replica_groups=mesh['xl'=2,'z'=8,'xh'=2,'y'=4,'c'=2] {'xh','xl','z'}, dimensions={0} | all-to-all | bytes 131072 | tf_op jit(solution)/shard_map/scores_all/all_to_all | solution.py:136
  37.5 0.6 %maximum_multiply_fusion = f32[4,256]{1,0:T(4,128)} fusion(f32[4,128]{1,0:T(4,128)S(1)} %get-tuple-element.10, f32[4,128]{1,0:T(4,128)S(1)} %get-tuple-element.9), kind=kLoop, calls=%fused_computation.6 | loop fusion | flops 2048 | bytes 8192 | tf_op jit(solution)/shard_map/mul | solution.py:140
  (5 shorter events, 0.1 us)
Async XLA Ops:
  0.0 14.3 %collective-permute-start.1 = (bf16[16,4096]{1,0:T(8,128)(2,1)}, bf16[16,4096]{1,0:T(8,128)(2,1)S(1)}, u32[]{:S(2)}, u32[]{:S(2)}) collective-permute-start(bf16[16,4096]{1,0:T(8,128)(2,1)} %bitcast.37), channel_id=1, source_target_pairs={{0,2},{2,0},{4,6},{6,4},{1,3},{3,1},{5,7},{7,5},{8,10},{10,8},{12,... | collective-permute-start | bytes 393224 | tf_op jit(solution)/shard_map/queries_y/ppermute | solution.py:103
  0.7 13.6 %collective-permute-start.2 = (bf16[16,4096]{1,0:T(8,128)(2,1)}, bf16[16,4096]{1,0:T(8,128)(2,1)S(1)}, u32[]{:S(2)}, u32[]{:S(2)}) collective-permute-start(bf16[16,4096]{1,0:T(8,128)(2,1)} %bitcast.38), channel_id=1, source_target_pairs={{0,4},{2,6},{4,0},{6,2},{1,5},{3,7},{5,1},{7,3},{8,12},{10,14},{12... | collective-permute-start | bytes 393224 | tf_op jit(solution)/shard_map/queries_y/ppermute | solution.py:103
  3.4 10.9 %collective-permute-start.3 = (bf16[16,4096]{1,0:T(8,128)(2,1)}, bf16[16,4096]{1,0:T(8,128)(2,1)S(1)}, u32[]{:S(2)}, u32[]{:S(2)}) collective-permute-start(bf16[16,4096]{1,0:T(8,128)(2,1)} %bitcast.39), channel_id=1, source_target_pairs={{0,6},{2,4},{4,2},{6,0},{1,7},{3,5},{5,3},{7,1},{8,14},{10,12},{12... | collective-permute-start | bytes 393224 | tf_op jit(solution)/shard_map/queries_y/ppermute | solution.py:103
  4.7 9.6 %copy-start = (bf16[1,16,4096]{2,1,0:T(8,128)(2,1)S(1)}, bf16[1,16,4096]{2,1,0:T(8,128)(2,1)}, u32[]{:S(2)}) copy-start(bf16[1,16,4096]{2,1,0:T(8,128)(2,1)} %param.10) | copy-start | bytes 393220
  10.0 5.5 %collective-permute-start = (bf16[4,4096]{1,0:T(4,128)(2,1)S(1)}, bf16[4,4096]{1,0:T(4,128)(2,1)S(1)}, u32[]{:S(2)}, u32[]{:S(2)}) collective-permute-start(bf16[4,4096]{1,0:T(4,128)(2,1)S(1)} %reshape.105), channel_id=1, source_target_pairs={{0,8},{8,0},{1,9},{9,1},{2,10},{10,2},{3,11},{11,3},{4,12},{12,4},... | collective-permute-start | bytes 98312 | tf_op jit(solution)/shard_map/projected_xh/ppermute | solution.py:103
  14.6 2.0 %collective-permute-start.4 = (bf16[4,16,4096]{2,1,0:T(8,128)(2,1)S(1)}, bf16[4,16,4096]{2,1,0:T(8,128)(2,1)S(1)}, u32[]{:S(2)}, u32[]{:S(2)}) collective-permute-start(bf16[4,16,4096]{2,1,0:T(8,128)(2,1)S(1)} %maximum_add_fusion.1), channel_id=1, source_target_pairs={{0,1},{1,0},{2,3},{3,2},{4,5},{5,4},{6,7},{7,6},{8,9},{9,8},{10,11... | collective-permute-start | bytes 1572872 | tf_op jit(solution)/shard_map/queries_core/ppermute | solution.py:103

commit v4 on v3

--- a/solution.py
+++ b/solution.py
@@ -116,8 +116,8 @@
         projected = project(activations, out_grads, proj_in, proj_out, lengths).reshape(-1, rank * rank)
     with jax.named_scope("projected_xh"):
         distant = exchange(projected, "xh", 1)
-    by_distance = jnp.stack([held[d] for d in range(len(held))])
-    along = jnp.stack([lax.dynamic_index_in_dim(by_distance, me ^ i, 0, False) for i in range(len(held))])
+    by_distance = jnp.stack([held[d] for d in reversed(range(len(held)))])
+    along = jnp.stack([lax.dynamic_index_in_dim(by_distance, len(held) - 1 - (me ^ i), 0, False) for i in range(len(held))])
     along = along + projected[0, 0] * 0
     with jax.named_scope("queries_core"):
         other = exchange(along, "c", 1)

time: 38.2 us -> 37.6 us (0.984)
  the two profiles are of different devices: /device:TPU:24 before, /device:TPU:16 now
where the time goes in v4:
time: 37.6 us; the launch traced here: 37.5 us
  blocking collectives  20.4 us (54%)
  starting transfers between devices  7.29 us (19%)
  Pallas kernels  5.21 us (14%)
  waiting for transfers between devices  1.72 us (5%)
  other arithmetic  1.02 us (3%)
  between operations  0.77 us (2%)
  local copies, waits for them, and re-layouts  0.74 us (2%)
  matrix products  0.39 us (1%)
    all_to_all x1, blocking collectives, body(): arrived = lax.all_to_all(spread, FINAL, 0, 0, tiled=True)  20.4 us
    ppermute x5, starting transfers between devices, exchange(): lax.ppermute(x, axis, [(i, i ^ distance) for i in range(lax.axis_size(axi...  7.29 us
    pallas_call x1, Pallas kernels, project(): pl.pallas_call(project_kernel, out_shape=pltpu.VMEM((examples, rank, rank...  5.21 us
    ppermute x5, waiting for transfers between devices, exchange(): lax.ppermute(x, axis, [(i, i ^ distance) for i in range(lax.axis_size(axi...  1.72 us
  transfers between devices with their start and end apart: 5, of which 2 were waited for; matrix products, arithmetic and copies ran while one was open for 3% of the time, Pallas kernels for 14%

profile of v4, /device:TPU:16, one launch (start us, length us, event | category | flops | bytes accessed | tf_op | source)
XLA Modules:
  0.0 37.5 jit_solution(5596829143380245410)
XLA Ops:
  0.0 0.4 %collective-permute-start.1 = (bf16[16,4096]{1,0:T(8,128)(2,1)}, bf16[16,4096]{1,0:T(8,128)(2,1)S(1)}, u32[]{:S(2)}, u32[]{:S(2)}) collective-permute-start(bf16[16,4096]{1,0:T(8,128)(2,1)} %bitcast.37), channel_id=1, source_target_pairs={{0,6},{2,4},{4,2},{6,0},{1,7},{3,5},{5,3},{7,1},{8,14},{10,12},{12... | collective-permute-start | bytes 393224 | tf_op jit(solution)/shard_map/queries_y/ppermute | solution.py:103
  0.5 2.9 %collective-permute-start.2 = (bf16[16,4096]{1,0:T(8,128)(2,1)}, bf16[16,4096]{1,0:T(8,128)(2,1)S(1)}, u32[]{:S(2)}, u32[]{:S(2)}) collective-permute-start(bf16[16,4096]{1,0:T(8,128)(2,1)} %bitcast.38), channel_id=1, source_target_pairs={{0,4},{2,6},{4,0},{6,2},{1,5},{3,7},{5,1},{7,3},{8,12},{10,14},{12... | collective-permute-start | bytes 393224 | tf_op jit(solution)/shard_map/queries_y/ppermute | solution.py:103
  3.4 0.7 %collective-permute-start.3 = (bf16[16,4096]{1,0:T(8,128)(2,1)}, bf16[16,4096]{1,0:T(8,128)(2,1)S(1)}, u32[]{:S(2)}, u32[]{:S(2)}) collective-permute-start(bf16[16,4096]{1,0:T(8,128)(2,1)} %bitcast.39), channel_id=1, source_target_pairs={{0,2},{2,0},{4,6},{6,4},{1,3},{3,1},{5,7},{7,5},{8,10},{10,8},{12,... | collective-permute-start | bytes 393224 | tf_op jit(solution)/shard_map/queries_y/ppermute | solution.py:103
  4.1 0.0 copy-start
  4.1 5.2 %project.1 = bf16[4,64,64]{2,1,0:T(8,128)(2,1)S(1)} custom-call(s32[1,4]{1,0:T(1,128)} %lengths_hbm.1, bf16[256,8192]{1,0:T(8,128)(2,1)} %bitcast.27, bf16[256,8192]{1,0:T(8,128)(2,1)} %bitcast.28, bf16[64,8192]{1,0:T(8,128)(2,1)} %bitcast.33, bf16[64,8192]{1,0:T(8,128)(2,1)} %bitcast.34), custom_call_target="tpu_custom_call" | custom-call | flops 536870912 | bytes 16777216 | tf_op jit(solution)/shard_map/project/project/pallas_call | solution.py:79
  9.3 0.1 reshape.105
  9.4 3.1 %collective-permute-start = (bf16[4,4096]{1,0:T(4,128)(2,1)S(1)}, bf16[4,4096]{1,0:T(4,128)(2,1)S(1)}, u32[]{:S(2)}, u32[]{:S(2)}) collective-permute-start(bf16[4,4096]{1,0:T(4,128)(2,1)S(1)} %reshape.105), channel_id=1, source_target_pairs={{0,8},{8,0},{1,9},{9,1},{2,10},{10,2},{3,11},{11,3},{4,12},{12,4},... | collective-permute-start | bytes 98312 | tf_op jit(solution)/shard_map/projected_xh/ppermute | solution.py:103
  12.5 0.5 %slice.12 = bf16[1,1]{1,0:T(2,128)(2,1)} slice(bf16[4,4096]{1,0:T(4,128)(2,1)S(1)} %reshape.105), slice={[0:1], [0:1]} | slice | bytes 4 | tf_op jit(solution)/shard_map/slice | solution.py:121
  13.7 0.0 collective-permute-done.1
  13.7 0.0 collective-permute-done.2
  13.7 0.0 collective-permute-done.3
  13.7 0.0 copy-done
  13.8 0.1 pad_maximum_fusion
  13.8 0.1 constant_dynamic-slice_fusion.3
  13.9 0.1 maximum_add_fusion.1
  14.0 0.1 collective-permute-start.4
  14.1 0.9 %collective-permute-done = bf16[4,4096]{1,0:T(4,128)(2,1)S(1)} collective-permute-done((bf16[4,4096]{1,0:T(4,128)(2,1)S(1)}, bf16[4,4096]{1,0:T(4,128)(2,1)S(1)}, u32[]{:S(2)}, u32[]{:S(2)}) %collective-permute-start) | collective-permute-done | bytes 32800 | tf_op jit(solution)/shard_map/projected_xh/ppermute | solution.py:103
  14.9 0.1 maximum_select_fusion.1
  15.0 0.1 maximum_add_fusion
  15.1 0.8 %collective-permute-done.4 = bf16[4,16,4096]{2,1,0:T(8,128)(2,1)S(1)} collective-permute-done((bf16[4,16,4096]{2,1,0:T(8,128)(2,1)S(1)}, bf16[4,16,4096]{2,1,0:T(8,128)(2,1)S(1)}, u32[]{:S(2)}, u32[]{:S(2)}) %collective-permute-start.4) | collective-permute-done | bytes 524320 | tf_op jit(solution)/shard_map/queries_core/ppermute | solution.py:103
  16.0 0.1 maximum_select_fusion
  16.1 0.4 %fusion = f32[2,4,128]{2,1,0:T(4,128)S(1)} fusion(bf16[2,4,4096]{2,1,0:T(4,128)(2,1)S(1)} %select_n.51, bf16[128,4096,1]{1,0,2:T(8,128)(2,1)S(1)} %bitcast.26), kind=kOutput, calls=%fused_computation.13 | convolution fusion | flops 8388608 | bytes 1118208 | tf_op jit(solution)/shard_map/dot_general | solution.py:129
  16.5 20.4 %all_to_all.5 = f32[32,4,128]{2,1,0:T(4,128)S(1)} all-to-all(f32[32,4,128]{2,1,0:T(4,128)S(1)} %bitcast.36), channel_id=1, replica_groups=mesh['xl'=2,'z'=8,'xh'=2,'y'=4,'c'=2] {'xh','xl','z'}, dimensions={0} | all-to-all | bytes 131072 | tf_op jit(solution)/shard_map/scores_all/all_to_all | solution.py:136
  36.9 0.6 %maximum_multiply_fusion = f32[4,256]{1,0:T(4,128)} fusion(f32[4,128]{1,0:T(4,128)S(1)} %get-tuple-element.10, f32[4,128]{1,0:T(4,128)S(1)} %get-tuple-element.9), kind=kLoop, calls=%fused_computation.6 | loop fusion | flops 2048 | bytes 8192 | tf_op jit(solution)/shard_map/mul | solution.py:140
  (4 shorter events, 0.1 us)
Async XLA Ops:
  0.0 13.7 %collective-permute-start.1 = (bf16[16,4096]{1,0:T(8,128)(2,1)}, bf16[16,4096]{1,0:T(8,128)(2,1)S(1)}, u32[]{:S(2)}, u32[]{:S(2)}) collective-permute-start(bf16[16,4096]{1,0:T(8,128)(2,1)} %bitcast.37), channel_id=1, source_target_pairs={{0,6},{2,4},{4,2},{6,0},{1,7},{3,5},{5,3},{7,1},{8,14},{10,12},{12... | collective-permute-start | bytes 393224 | tf_op jit(solution)/shard_map/queries_y/ppermute | solution.py:103
  0.5 13.3 %collective-permute-start.2 = (bf16[16,4096]{1,0:T(8,128)(2,1)}, bf16[16,4096]{1,0:T(8,128)(2,1)S(1)}, u32[]{:S(2)}, u32[]{:S(2)}) collective-permute-start(bf16[16,4096]{1,0:T(8,128)(2,1)} %bitcast.38), channel_id=1, source_target_pairs={{0,4},{2,6},{4,0},{6,2},{1,5},{3,7},{5,1},{7,3},{8,12},{10,14},{12... | collective-permute-start | bytes 393224 | tf_op jit(solution)/shard_map/queries_y/ppermute | solution.py:103
  3.4 10.4 %collective-permute-start.3 = (bf16[16,4096]{1,0:T(8,128)(2,1)}, bf16[16,4096]{1,0:T(8,128)(2,1)S(1)}, u32[]{:S(2)}, u32[]{:S(2)}) collective-permute-start(bf16[16,4096]{1,0:T(8,128)(2,1)} %bitcast.39), channel_id=1, source_target_pairs={{0,2},{2,0},{4,6},{6,4},{1,3},{3,1},{5,7},{7,5},{8,10},{10,8},{12,... | collective-permute-start | bytes 393224 | tf_op jit(solution)/shard_map/queries_y/ppermute | solution.py:103
  4.1 9.6 %copy-start = (bf16[1,16,4096]{2,1,0:T(8,128)(2,1)S(1)}, bf16[1,16,4096]{2,1,0:T(8,128)(2,1)}, u32[]{:S(2)}) copy-start(bf16[1,16,4096]{2,1,0:T(8,128)(2,1)} %param.10) | copy-start | bytes 393220
  9.4 5.5 %collective-permute-start = (bf16[4,4096]{1,0:T(4,128)(2,1)S(1)}, bf16[4,4096]{1,0:T(4,128)(2,1)S(1)}, u32[]{:S(2)}, u32[]{:S(2)}) collective-permute-start(bf16[4,4096]{1,0:T(4,128)(2,1)S(1)} %reshape.105), channel_id=1, source_target_pairs={{0,8},{8,0},{1,9},{9,1},{2,10},{10,2},{3,11},{11,3},{4,12},{12,4},... | collective-permute-start | bytes 98312 | tf_op jit(solution)/shard_map/projected_xh/ppermute | solution.py:103
  14.0 2.0 %collective-permute-start.4 = (bf16[4,16,4096]{2,1,0:T(8,128)(2,1)S(1)}, bf16[4,16,4096]{2,1,0:T(8,128)(2,1)S(1)}, u32[]{:S(2)}, u32[]{:S(2)}) collective-permute-start(bf16[4,16,4096]{2,1,0:T(8,128)(2,1)S(1)} %maximum_add_fusion.1), channel_id=1, source_target_pairs={{0,1},{1,0},{2,3},{3,2},{4,5},{5,4},{6,7},{7,6},{8,9},{9,8},{10,11... | collective-permute-start | bytes 1572872 | tf_op jit(solution)/shard_map/queries_core/ppermute | solution.py:103

commit v5 on v4

--- a/solution.py
+++ b/solution.py
@@ -6,8 +6,9 @@
 from jax.sharding import Mesh, PartitionSpec as P
 
 SECTION = ("xl", "z")
-GROUP = ("xh", "y", "c")
-FINAL = ("xh", "xl", "z")
+GROUP = ("xh", "yh", "yl", "c")
+NEAR = ("xh", "yh")
+FINAL = ("yl", "xl", "z")
 STEPS = 8
 AHEAD = 4
 ORDER = (1, 2, 3)
@@ -108,14 +109,14 @@
     slots = activations.shape[2]
     own = queries[0]
     with jax.named_scope("queries_y"):
-        me = lax.axis_index("y")
+        me = lax.axis_index(NEAR)
         held = {0: own}
         for distance in ORDER:
-            held[distance] = exchange(own, "y", distance)
+            held[distance] = exchange(own, NEAR, distance)
     with jax.named_scope("project"):
         projected = project(activations, out_grads, proj_in, proj_out, lengths).reshape(-1, rank * rank)
     with jax.named_scope("projected_xh"):
-        distant = exchange(projected, "xh", 1)
+        distant = exchange(projected, "yl", 1)
     by_distance = jnp.stack([held[d] for d in reversed(range(len(held)))])
     along = jnp.stack([lax.dynamic_index_in_dim(by_distance, len(held) - 1 - (me ^ i), 0, False) for i in range(len(held))])
     along = along + projected[0, 0] * 0
@@ -124,12 +125,12 @@
     first = lax.axis_index("c") == 0
     stored = jnp.where(first, jnp.stack([along, other], 1), jnp.stack([other, along], 1))
     stored = stored.reshape(-1, own.shape[-1])
-    low = lax.axis_index("xh") == 0
+    low = lax.axis_index("yl") == 0
     pair = jnp.where(low, jnp.concatenate([projected, distant]), jnp.concatenate([distant, projected]))
     partial = lax.dot_general(pair, stored, BOTH_LAST, preferred_element_type=jnp.float32)
     sections = lax.axis_size(SECTION)
     sizes = [lax.axis_size(axis) for axis in FINAL]
-    at = FINAL.index("xh")
+    at = FINAL.index("yl")
     partial = partial.reshape([2 if i == at else 1 for i in range(3)] + [projected.shape[0], -1])
     spread = jnp.broadcast_to(partial, tuple(sizes) + partial.shape[3:]).reshape((-1,) + partial.shape[3:])
     with jax.named_scope("scores_all"):
@@ -137,11 +138,13 @@
     arrived = arrived.reshape(tuple(sizes) + arrived.shape[1:])
     summed = arrived.sum([i for i in range(3) if i != at])
     norm_factor = 1.0 / (rank * (slots * sections) ** 0.5)
-    return jnp.concatenate([summed[0], summed[1]], axis=1) * norm_factor
+    near = lax.axis_size(NEAR)
+    blocks = [half.reshape(half.shape[0], near, 1, -1) for half in (summed[0], summed[1])]
+    return jnp.concatenate(blocks, axis=2).reshape(projected.shape[0], -1) * norm_factor
 
 
 def solution(mesh):
-    fine = Mesh(mesh.devices.reshape(2, 8, 2, 4, 2), SECTION + GROUP)
+    fine = Mesh(mesh.devices.reshape(2, 8, 2, 2, 2, 2), SECTION + GROUP)
     placed = (
         P(SECTION, GROUP, None, None),
         P(SECTION, GROUP, None, None),

time: 37.6 us -> 37.4 us (level)
  the two profiles are of different devices: /device:TPU:16 before, /device:TPU:2 now
where the time goes in v5:
time: 37.4 us; the launch traced here: 36.7 us
  blocking collectives  18.3 us (49%)
  starting transfers between devices  8.25 us (22%)
  Pallas kernels  5.21 us (14%)
  waiting for transfers between devices  1.72 us (5%)
  local copies, waits for them, and re-layouts  1.6 us (4%)
  between operations  0.78 us (2%)
  other arithmetic  0.43 us (1%)
  matrix products  0.39 us (1%)
    all_to_all x1, blocking collectives, body(): arrived = lax.all_to_all(spread, FINAL, 0, 0, tiled=True)  18.3 us
    ppermute x5, starting transfers between devices, exchange(): lax.ppermute(x, axis, [(i, i ^ distance) for i in range(lax.axis_size(axi...  8.25 us
    pallas_call x1, Pallas kernels, project(): pl.pallas_call(project_kernel, out_shape=pltpu.VMEM((examples, rank, rank...  5.21 us
    ppermute x5, waiting for transfers between devices, exchange(): lax.ppermute(x, axis, [(i, i ^ distance) for i in range(lax.axis_size(axi...  1.72 us
  transfers between devices with their start and end apart: 5, of which 2 were waited for; matrix products, arithmetic and copies ran while one was open for 3% of the time, Pallas kernels for 14%

profile of v5, /device:TPU:2, one launch (start us, length us, event | category | flops | bytes accessed | tf_op | source)
XLA Modules:
  0.0 36.7 jit_solution(12948394483191179418)
XLA Ops:
  0.0 4.8 %collective-permute-start.1 = (bf16[16,4096]{1,0:T(8,128)(2,1)}, bf16[16,4096]{1,0:T(8,128)(2,1)S(1)}, u32[]{:S(2)}, u32[]{:S(2)}) collective-permute-start(bf16[16,4096]{1,0:T(8,128)(2,1)} %bitcast.33), channel_id=1, source_target_pairs={{0,12},{4,8},{8,4},{12,0},{1,13},{5,9},{9,5},{13,1},{2,14},{6,10},... | collective-permute-start | bytes 393224 | tf_op jit(solution)/shard_map/queries_y/ppermute | solution.py:104
  4.8 1.4 %collective-permute-start.2 = (bf16[16,4096]{1,0:T(8,128)(2,1)}, bf16[16,4096]{1,0:T(8,128)(2,1)S(1)}, u32[]{:S(2)}, u32[]{:S(2)}) collective-permute-start(bf16[16,4096]{1,0:T(8,128)(2,1)} %bitcast.34), channel_id=1, source_target_pairs={{0,8},{4,12},{8,0},{12,4},{1,9},{5,13},{9,1},{13,5},{2,10},{6,14},... | collective-permute-start | bytes 393224 | tf_op jit(solution)/shard_map/queries_y/ppermute | solution.py:104
  6.2 0.3 collective-permute-start.3
  6.5 0.0 copy-start
  6.5 5.2 %project.1 = bf16[4,64,64]{2,1,0:T(8,128)(2,1)S(1)} custom-call(s32[1,4]{1,0:T(1,128)} %lengths_hbm.1, bf16[256,8192]{1,0:T(8,128)(2,1)} %bitcast.23, bf16[256,8192]{1,0:T(8,128)(2,1)} %bitcast.24, bf16[64,8192]{1,0:T(8,128)(2,1)} %bitcast.29, bf16[64,8192]{1,0:T(8,128)(2,1)} %bitcast.30), custom_call_target="tpu_custom_call" | custom-call | flops 536870912 | bytes 16777216 | tf_op jit(solution)/shard_map/project/project/pallas_call | solution.py:80
  11.7 0.1 reshape.108
  11.8 1.7 %collective-permute-start = (bf16[4,4096]{1,0:T(4,128)(2,1)S(1)}, bf16[4,4096]{1,0:T(4,128)(2,1)S(1)}, u32[]{:S(2)}, u32[]{:S(2)}) collective-permute-start(bf16[4,4096]{1,0:T(4,128)(2,1)S(1)} %reshape.108), channel_id=1, source_target_pairs={{0,2},{2,0},{1,3},{3,1},{4,6},{6,4},{5,7},{7,5},{8,10},{10,8},{9,1... | collective-permute-start | bytes 98312 | tf_op jit(solution)/shard_map/projected_xh/ppermute | solution.py:104
  13.5 0.5 %slice.12 = bf16[1,1]{1,0:T(2,128)(2,1)} slice(bf16[4,4096]{1,0:T(4,128)(2,1)S(1)} %reshape.108), slice={[0:1], [0:1]} | slice | bytes 4 | tf_op jit(solution)/shard_map/slice | solution.py:122
  14.7 0.0 collective-permute-done.1
  14.7 0.0 collective-permute-done.2
  14.7 0.0 collective-permute-done.3
  14.7 0.0 copy-done
  14.7 0.1 pad_maximum_fusion
  14.8 0.1 maximum_add_fusion.1
  14.9 0.1 collective-permute-start.4
  15.0 0.8 %collective-permute-done = bf16[4,4096]{1,0:T(4,128)(2,1)S(1)} collective-permute-done((bf16[4,4096]{1,0:T(4,128)(2,1)S(1)}, bf16[4,4096]{1,0:T(4,128)(2,1)S(1)}, u32[]{:S(2)}, u32[]{:S(2)}) %collective-permute-start) | collective-permute-done | bytes 32800 | tf_op jit(solution)/shard_map/projected_xh/ppermute | solution.py:104
  15.8 0.1 maximum_select_fusion.1
  15.9 0.1 maximum_add_fusion
  16.0 0.9 %collective-permute-done.4 = bf16[4,16,4096]{2,1,0:T(8,128)(2,1)S(1)} collective-permute-done((bf16[4,16,4096]{2,1,0:T(8,128)(2,1)S(1)}, bf16[4,16,4096]{2,1,0:T(8,128)(2,1)S(1)}, u32[]{:S(2)}, u32[]{:S(2)}) %collective-permute-start.4) | collective-permute-done | bytes 524320 | tf_op jit(solution)/shard_map/queries_core/ppermute | solution.py:104
  16.9 0.1 maximum_select_fusion
  17.0 0.4 %fusion.1 = f32[2,4,128]{2,1,0:T(4,128)S(1)} fusion(bf16[2,4,4096]{2,1,0:T(4,128)(2,1)S(1)} %select_n.51, bf16[128,4096,1]{1,0,2:T(8,128)(2,1)S(1)} %bitcast.22), kind=kOutput, calls=%fused_computation.12 | convolution fusion | flops 8388608 | bytes 1118208 | tf_op jit(solution)/shard_map/dot_general | solution.py:130
  17.5 18.3 %all_to_all.5 = f32[32,4,128]{2,1,0:T(4,128)S(1)} all-to-all(f32[32,4,128]{2,1,0:T(4,128)S(1)} %bitcast.32), channel_id=1, replica_groups=mesh['xl'=2,'z'=8,'xh'=2,'yh'=2,'yl'=2,'c'=2] {'yl','xl','z'}, dimensions={0} | all-to-all | bytes 131072 | tf_op jit(solution)/shard_map/scores_all/all_to_all | solution.py:137
  35.8 0.1 reshape_squeeze.6
  35.9 0.1 reshape_squeeze.7
  36.0 0.7 %mul.23 = f32[4,256]{1,0:T(4,128)} reshape(f32[4,4,2,32]{3,2,1,0:T(2,128)S(1)} %copy.13) | data formatting | bytes 8192 | tf_op jit(solution)/shard_map/mul | solution.py:143
  (7 shorter events, 0.2 us)
Async XLA Ops:
  0.0 14.7 %collective-permute-start.1 = (bf16[16,4096]{1,0:T(8,128)(2,1)}, bf16[16,4096]{1,0:T(8,128)(2,1)S(1)}, u32[]{:S(2)}, u32[]{:S(2)}) collective-permute-start(bf16[16,4096]{1,0:T(8,128)(2,1)} %bitcast.33), channel_id=1, source_target_pairs={{0,12},{4,8},{8,4},{12,0},{1,13},{5,9},{9,5},{13,1},{2,14},{6,10},... | collective-permute-start | bytes 393224 | tf_op jit(solution)/shard_map/queries_y/ppermute | solution.py:104
  4.8 9.9 %collective-permute-start.2 = (bf16[16,4096]{1,0:T(8,128)(2,1)}, bf16[16,4096]{1,0:T(8,128)(2,1)S(1)}, u32[]{:S(2)}, u32[]{:S(2)}) collective-permute-start(bf16[16,4096]{1,0:T(8,128)(2,1)} %bitcast.34), channel_id=1, source_target_pairs={{0,8},{4,12},{8,0},{12,4},{1,9},{5,13},{9,1},{13,5},{2,10},{6,14},... | collective-permute-start | bytes 393224 | tf_op jit(solution)/shard_map/queries_y/ppermute | solution.py:104
  6.2 8.5 %collective-permute-start.3 = (bf16[16,4096]{1,0:T(8,128)(2,1)}, bf16[16,4096]{1,0:T(8,128)(2,1)S(1)}, u32[]{:S(2)}, u32[]{:S(2)}) collective-permute-start(bf16[16,4096]{1,0:T(8,128)(2,1)} %bitcast.35), channel_id=1, source_target_pairs={{0,4},{4,0},{8,12},{12,8},{1,5},{5,1},{9,13},{13,9},{2,6},{6,2},{1... | collective-permute-start | bytes 393224 | tf_op jit(solution)/shard_map/queries_y/ppermute | solution.py:104
  6.5 8.2 %copy-start = (bf16[1,16,4096]{2,1,0:T(8,128)(2,1)S(1)}, bf16[1,16,4096]{2,1,0:T(8,128)(2,1)}, u32[]{:S(2)}) copy-start(bf16[1,16,4096]{2,1,0:T(8,128)(2,1)} %param.10) | copy-start | bytes 393220
  11.8 4.0 %collective-permute-start = (bf16[4,4096]{1,0:T(4,128)(2,1)S(1)}, bf16[4,4096]{1,0:T(4,128)(2,1)S(1)}, u32[]{:S(2)}, u32[]{:S(2)}) collective-permute-start(bf16[4,4096]{1,0:T(4,128)(2,1)S(1)} %reshape.108), channel_id=1, source_target_pairs={{0,2},{2,0},{1,3},{3,1},{4,6},{6,4},{5,7},{7,5},{8,10},{10,8},{9,1... | collective-permute-start | bytes 98312 | tf_op jit(solution)/shard_map/projected_xh/ppermute | solution.py:104
  14.9 2.0 %collective-permute-start.4 = (bf16[4,16,4096]{2,1,0:T(8,128)(2,1)S(1)}, bf16[4,16,4096]{2,1,0:T(8,128)(2,1)S(1)}, u32[]{:S(2)}, u32[]{:S(2)}) collective-permute-start(bf16[4,16,4096]{2,1,0:T(8,128)(2,1)S(1)} %maximum_add_fusion.1), channel_id=1, source_target_pairs={{0,1},{1,0},{2,3},{3,2},{4,5},{5,4},{6,7},{7,6},{8,9},{9,8},{10,11... | collective-permute-start | bytes 1572872 | tf_op jit(solution)/shard_map/queries_core/ppermute | solution.py:104

commit v6 on v5

--- a/solution.py
+++ b/solution.py
@@ -117,8 +117,8 @@
         projected = project(activations, out_grads, proj_in, proj_out, lengths).reshape(-1, rank * rank)
     with jax.named_scope("projected_xh"):
         distant = exchange(projected, "yl", 1)
-    by_distance = jnp.stack([held[d] for d in reversed(range(len(held)))])
-    along = jnp.stack([lax.dynamic_index_in_dim(by_distance, len(held) - 1 - (me ^ i), 0, False) for i in range(len(held))])
+    by_distance = jnp.stack([held[d] for d in (1, 2, 3, 0)])
+    along = jnp.stack([lax.dynamic_index_in_dim(by_distance, lax.rem((me ^ i) + 3, 4), 0, False) for i in range(len(held))])
     along = along + projected[0, 0] * 0
     with jax.named_scope("queries_core"):
         other = exchange(along, "c", 1)

time: 37.4 us -> 37.4 us (level)
  no operation moved by 1% of the time
where the time goes in v6:
time: 37.4 us; the launch traced here: 36.7 us
  blocking collectives  18.3 us (49%)
  starting transfers between devices  8.25 us (22%)
  Pallas kernels  5.21 us (14%)
  waiting for transfers between devices  1.72 us (5%)
  local copies, waits for them, and re-layouts  1.59 us (4%)
  between operations  0.78 us (2%)
  other arithmetic  0.43 us (1%)
  matrix products  0.39 us (1%)
    all_to_all x1, blocking collectives, body(): arrived = lax.all_to_all(spread, FINAL, 0, 0, tiled=True)  18.3 us
    ppermute x5, starting transfers between devices, exchange(): lax.ppermute(x, axis, [(i, i ^ distance) for i in range(lax.axis_size(axi...  8.25 us
    pallas_call x1, Pallas kernels, project(): pl.pallas_call(project_kernel, out_shape=pltpu.VMEM((examples, rank, rank...  5.21 us
    ppermute x5, waiting for transfers between devices, exchange(): lax.ppermute(x, axis, [(i, i ^ distance) for i in range(lax.axis_size(axi...  1.72 us
  transfers between devices with their start and end apart: 5, of which 2 were waited for; matrix products, arithmetic and copies ran while one was open for 3% of the time, Pallas kernels for 14%

profile of v6, /device:TPU:2, one launch (start us, length us, event | category | flops | bytes accessed | tf_op | source)
XLA Modules:
  0.0 36.7 jit_solution(13693399857301937612)
XLA Ops:
  0.0 3.2 %collective-permute-start.1 = (bf16[16,4096]{1,0:T(8,128)(2,1)}, bf16[16,4096]{1,0:T(8,128)(2,1)S(1)}, u32[]{:S(2)}, u32[]{:S(2)}) collective-permute-start(bf16[16,4096]{1,0:T(8,128)(2,1)} %bitcast.33), channel_id=1, source_target_pairs={{0,4},{4,0},{8,12},{12,8},{1,5},{5,1},{9,13},{13,9},{2,6},{6,2},{1... | collective-permute-start | bytes 393224 | tf_op jit(solution)/shard_map/queries_y/ppermute | solution.py:104
  3.2 2.1 %collective-permute-start.2 = (bf16[16,4096]{1,0:T(8,128)(2,1)}, bf16[16,4096]{1,0:T(8,128)(2,1)S(1)}, u32[]{:S(2)}, u32[]{:S(2)}) collective-permute-start(bf16[16,4096]{1,0:T(8,128)(2,1)} %bitcast.34), channel_id=1, source_target_pairs={{0,8},{4,12},{8,0},{12,4},{1,9},{5,13},{9,1},{13,5},{2,10},{6,14},... | collective-permute-start | bytes 393224 | tf_op jit(solution)/shard_map/queries_y/ppermute | solution.py:104
  5.3 1.2 %collective-permute-start.3 = (bf16[16,4096]{1,0:T(8,128)(2,1)}, bf16[16,4096]{1,0:T(8,128)(2,1)S(1)}, u32[]{:S(2)}, u32[]{:S(2)}) collective-permute-start(bf16[16,4096]{1,0:T(8,128)(2,1)} %bitcast.35), channel_id=1, source_target_pairs={{0,12},{4,8},{8,4},{12,0},{1,13},{5,9},{9,5},{13,1},{2,14},{6,10},... | collective-permute-start | bytes 393224 | tf_op jit(solution)/shard_map/queries_y/ppermute | solution.py:104
  6.5 0.0 copy-start
  6.5 5.2 %project.1 = bf16[4,64,64]{2,1,0:T(8,128)(2,1)S(1)} custom-call(s32[1,4]{1,0:T(1,128)} %lengths_hbm.1, bf16[256,8192]{1,0:T(8,128)(2,1)} %bitcast.23, bf16[256,8192]{1,0:T(8,128)(2,1)} %bitcast.24, bf16[64,8192]{1,0:T(8,128)(2,1)} %bitcast.29, bf16[64,8192]{1,0:T(8,128)(2,1)} %bitcast.30), custom_call_target="tpu_custom_call" | custom-call | flops 536870912 | bytes 16777216 | tf_op jit(solution)/shard_map/project/project/pallas_call | solution.py:80
  11.7 0.1 reshape.108
  11.8 1.7 %collective-permute-start = (bf16[4,4096]{1,0:T(4,128)(2,1)S(1)}, bf16[4,4096]{1,0:T(4,128)(2,1)S(1)}, u32[]{:S(2)}, u32[]{:S(2)}) collective-permute-start(bf16[4,4096]{1,0:T(4,128)(2,1)S(1)} %reshape.108), channel_id=1, source_target_pairs={{0,2},{2,0},{1,3},{3,1},{4,6},{6,4},{5,7},{7,5},{8,10},{10,8},{9,1... | collective-permute-start | bytes 98312 | tf_op jit(solution)/shard_map/projected_xh/ppermute | solution.py:104
  13.5 0.5 %slice.12 = bf16[1,1]{1,0:T(2,128)(2,1)} slice(bf16[4,4096]{1,0:T(4,128)(2,1)S(1)} %reshape.108), slice={[0:1], [0:1]} | slice | bytes 4 | tf_op jit(solution)/shard_map/slice | solution.py:122
  14.7 0.0 collective-permute-done.1
  14.7 0.0 collective-permute-done.2
  14.7 0.0 collective-permute-done.3
  14.7 0.0 copy-done
  14.7 0.1 pad_maximum_fusion
  14.8 0.1 maximum_add_fusion.1
  14.9 0.1 collective-permute-start.4
  15.0 0.8 %collective-permute-done = bf16[4,4096]{1,0:T(4,128)(2,1)S(1)} collective-permute-done((bf16[4,4096]{1,0:T(4,128)(2,1)S(1)}, bf16[4,4096]{1,0:T(4,128)(2,1)S(1)}, u32[]{:S(2)}, u32[]{:S(2)}) %collective-permute-start) | collective-permute-done | bytes 32800 | tf_op jit(solution)/shard_map/projected_xh/ppermute | solution.py:104
  15.8 0.1 maximum_select_fusion.1
  15.9 0.1 maximum_add_fusion
  16.0 0.9 %collective-permute-done.4 = bf16[4,16,4096]{2,1,0:T(8,128)(2,1)S(1)} collective-permute-done((bf16[4,16,4096]{2,1,0:T(8,128)(2,1)S(1)}, bf16[4,16,4096]{2,1,0:T(8,128)(2,1)S(1)}, u32[]{:S(2)}, u32[]{:S(2)}) %collective-permute-start.4) | collective-permute-done | bytes 524320 | tf_op jit(solution)/shard_map/queries_core/ppermute | solution.py:104
  16.9 0.1 maximum_select_fusion
  17.0 0.4 %fusion.1 = f32[2,4,128]{2,1,0:T(4,128)S(1)} fusion(bf16[2,4,4096]{2,1,0:T(4,128)(2,1)S(1)} %select_n.51, bf16[128,4096,1]{1,0,2:T(8,128)(2,1)S(1)} %bitcast.22), kind=kOutput, calls=%fused_computation.12 | convolution fusion | flops 8388608 | bytes 1118208 | tf_op jit(solution)/shard_map/dot_general | solution.py:130
  17.5 18.3 %all_to_all.5 = f32[32,4,128]{2,1,0:T(4,128)S(1)} all-to-all(f32[32,4,128]{2,1,0:T(4,128)S(1)} %bitcast.32), channel_id=1, replica_groups=mesh['xl'=2,'z'=8,'xh'=2,'yh'=2,'yl'=2,'c'=2] {'yl','xl','z'}, dimensions={0} | all-to-all | bytes 131072 | tf_op jit(solution)/shard_map/scores_all/all_to_all | solution.py:137
  35.8 0.1 reshape_squeeze.6
  35.9 0.1 reshape_squeeze.7
  36.0 0.7 %mul.23 = f32[4,256]{1,0:T(4,128)} reshape(f32[4,4,2,32]{3,2,1,0:T(2,128)S(1)} %copy.13) | data formatting | bytes 8192 | tf_op jit(solution)/shard_map/mul | solution.py:143
  (7 shorter events, 0.2 us)
Async XLA Ops:
  0.0 14.7 %collective-permute-start.1 = (bf16[16,4096]{1,0:T(8,128)(2,1)}, bf16[16,4096]{1,0:T(8,128)(2,1)S(1)}, u32[]{:S(2)}, u32[]{:S(2)}) collective-permute-start(bf16[16,4096]{1,0:T(8,128)(2,1)} %bitcast.33), channel_id=1, source_target_pairs={{0,4},{4,0},{8,12},{12,8},{1,5},{5,1},{9,13},{13,9},{2,6},{6,2},{1... | collective-permute-start | bytes 393224 | tf_op jit(solution)/shard_map/queries_y/ppermute | solution.py:104
  3.2 11.5 %collective-permute-start.2 = (bf16[16,4096]{1,0:T(8,128)(2,1)}, bf16[16,4096]{1,0:T(8,128)(2,1)S(1)}, u32[]{:S(2)}, u32[]{:S(2)}) collective-permute-start(bf16[16,4096]{1,0:T(8,128)(2,1)} %bitcast.34), channel_id=1, source_target_pairs={{0,8},{4,12},{8,0},{12,4},{1,9},{5,13},{9,1},{13,5},{2,10},{6,14},... | collective-permute-start | bytes 393224 | tf_op jit(solution)/shard_map/queries_y/ppermute | solution.py:104
  5.3 9.4 %collective-permute-start.3 = (bf16[16,4096]{1,0:T(8,128)(2,1)}, bf16[16,4096]{1,0:T(8,128)(2,1)S(1)}, u32[]{:S(2)}, u32[]{:S(2)}) collective-permute-start(bf16[16,4096]{1,0:T(8,128)(2,1)} %bitcast.35), channel_id=1, source_target_pairs={{0,12},{4,8},{8,4},{12,0},{1,13},{5,9},{9,5},{13,1},{2,14},{6,10},... | collective-permute-start | bytes 393224 | tf_op jit(solution)/shard_map/queries_y/ppermute | solution.py:104
  6.5 8.2 %copy-start = (bf16[1,16,4096]{2,1,0:T(8,128)(2,1)S(1)}, bf16[1,16,4096]{2,1,0:T(8,128)(2,1)}, u32[]{:S(2)}) copy-start(bf16[1,16,4096]{2,1,0:T(8,128)(2,1)} %param.10) | copy-start | bytes 393220
  11.8 4.0 %collective-permute-start = (bf16[4,4096]{1,0:T(4,128)(2,1)S(1)}, bf16[4,4096]{1,0:T(4,128)(2,1)S(1)}, u32[]{:S(2)}, u32[]{:S(2)}) collective-permute-start(bf16[4,4096]{1,0:T(4,128)(2,1)S(1)} %reshape.108), channel_id=1, source_target_pairs={{0,2},{2,0},{1,3},{3,1},{4,6},{6,4},{5,7},{7,5},{8,10},{10,8},{9,1... | collective-permute-start | bytes 98312 | tf_op jit(solution)/shard_map/projected_xh/ppermute | solution.py:104
  14.9 2.0 %collective-permute-start.4 = (bf16[4,16,4096]{2,1,0:T(8,128)(2,1)S(1)}, bf16[4,16,4096]{2,1,0:T(8,128)(2,1)S(1)}, u32[]{:S(2)}, u32[]{:S(2)}) collective-permute-start(bf16[4,16,4096]{2,1,0:T(8,128)(2,1)S(1)} %maximum_add_fusion.1), channel_id=1, source_target_pairs={{0,1},{1,0},{2,3},{3,2},{4,5},{5,4},{6,7},{7,6},{8,9},{9,8},{10,11... | collective-permute-start | bytes 1572872 | tf_op jit(solution)/shard_map/queries_core/ppermute | solution.py:104
